TPU v7x, 128 devices: a whole 4x4x4 slice. The times are simulated.
128 devices in a mesh: dp: 32 (over z_lo, x, y), mp: 4 (over z_hi, core).
Axes of the slice: x: 4, y: 4, z: 4 (z_hi: 2, z_lo: 2; z = z_hi * 2 + z_lo), core: 2. Of those that a mesh axis runs over, the one named last changes fastest.
Arguments:
- tokens: bfloat16 [32768, 8192], P('dp'), may hold values from -500 to 500
- norm_gain: bfloat16 [8192], replicated, may hold values from 0.099609375 to 1.8984375
- query_weight: bfloat16 [8192, 4096], P('dp', 'mp'), may hold values from -0.0625 to 0.0625
- query_bias: bfloat16 [4096], P('mp'), may hold values from -3 to 3
- keyval_weight: bfloat16 [8192, 4, 256], P('dp', 'mp'), may hold values from -0.0625 to 0.0625
- keyval_bias: bfloat16 [4, 256], P('mp'), may hold values from -4 to 4
- visual_keyval: bfloat16 [32, 1024, 4, 256], P('dp', 'mp'), may hold values from -70 to 70
- caption_image: int32 [512], P('dp'), may hold values from 0 to 31, as said below
- caption_length: int32 [512], P('dp'), may hold values from 1 to 64
- image_owner: int32 [32], replicated, may hold values from 0 to 31, each once
Outputs:
- attended: bfloat16 [32768, 4096], P('dp', 'mp')
Inputs may be any that keep to these rules, and one draw needn't show every extreme that they name: `caption_image`: Non-decreasing; caption c has image c // 16 or the image before it; image 0 starts at caption 0 and every later image i starts at a caption between i * 16 + 1 and i * 16 + 16 // 2, so every image has between 8 and 24 captions. `image_owner`: each row of visual_keyval holds exactly one image.
All inputs are finite; a program needn't handle non-finite values.
Results may differ from a plain program's by a relative error of at most 0.0049.
The roundings to bfloat16 on the way count: a program that leaves them out, or rounds other values in their place, can miss the bound.
Values may be sent and summed in bfloat16 or wider, within the bound.
No kernel may reach another device: no remote copies, remote signals or barrier semaphores. Data moves between devices by JAX's collectives and lax.ppermute only.
A program may use at most 192 MiB of HBM per device.

v0:
```python
import jax
import jax.numpy as jnp
from jax import lax
from jax.sharding import PartitionSpec as P

ROPE_BASE = 1000000.0


def rotate(values_in, positions):
    half_width = values_in.shape[-1] // 2
    freqs = ROPE_BASE ** (-jnp.arange(half_width, dtype=jnp.float32) / half_width)
    angles = positions[:, None] * freqs[None, :]
    target = (positions.shape[0],) + (1,) * (values_in.ndim - 3) + (half_width,)
    cosine = jnp.cos(angles).reshape(target)
    sine_part = jnp.sin(angles).reshape(target)
    first = values_in[..., :half_width]
    second = values_in[..., half_width:]
    return jnp.concatenate(
        [first * cosine - second * sine_part, second * cosine + first * sine_part], -1
    )


def on_device(
    tokens,
    norm_gain,
    query_weight,
    query_bias,
    keyval_weight,
    keyval_bias,
    visual_keyval,
    caption_image,
    caption_length,
    image_owner,
):
    captions = caption_image.shape[0]
    row_count = tokens.shape[0]
    cap_length = row_count // captions
    head_dim = keyval_weight.shape[2] // 2
    local_kv = keyval_weight.shape[1]
    local_heads = query_bias.shape[0] // head_dim
    group_size = local_heads // local_kv
    widened = tokens.astype(jnp.float32)
    mean_square = jnp.mean(widened * widened, -1, keepdims=True)
    normed = (widened * lax.rsqrt(mean_square + 1e-06) * norm_gain.astype(jnp.float32)).astype(
        jnp.bfloat16
    )
    visual = lax.all_to_all(visual_keyval, "mp", split_axis=2, concat_axis=1, tiled=True)
    image_count = image_owner.shape[0]
    image_range = jnp.arange(image_count, dtype=jnp.int32)
    image_match = caption_image[:, None] == image_range[None, :]
    owner_of = jnp.sum(jnp.where(image_match, image_owner[None, :], 0), axis=1)
    gathered = lax.all_gather(visual, "dp", axis=0, tiled=True)
    owner_range = jnp.arange(gathered.shape[0], dtype=jnp.int32)
    selector = (owner_of[:, None] == owner_range[None, :]).astype(jnp.bfloat16)
    picked = jnp.einsum(
        "cn,nsgd->csgd", selector, gathered, preferred_element_type=jnp.float32
    ).astype(jnp.bfloat16)

    def add_part(shard_piece):
        flat_piece = shard_piece.reshape(shard_piece.shape[0], -1)
        return jnp.dot(normed, flat_piece, preferred_element_type=jnp.float32)

    query_full = add_part(lax.all_gather(query_weight, "dp", axis=0, tiled=True))
    keyval = add_part(lax.all_gather(keyval_weight, "dp", axis=0, tiled=True))
    query_full = query_full + query_bias.astype(jnp.float32)
    keyval = keyval + keyval_bias.reshape(-1).astype(jnp.float32)
    query_full = query_full.reshape(captions, cap_length, local_kv, group_size, head_dim)
    keyval = keyval.reshape(captions, cap_length, local_kv, 2 * head_dim)
    vis_tokens = picked.shape[1]
    positions = (vis_tokens + jnp.arange(cap_length, dtype=jnp.int32)).astype(jnp.float32)
    query_rot = rotate(query_full, positions).astype(jnp.bfloat16)
    key_text = rotate(keyval[..., :head_dim], positions).astype(jnp.bfloat16)
    value_text = keyval[..., head_dim:].astype(jnp.bfloat16)
    score_scale = 1.0 / jnp.sqrt(jnp.float32(head_dim))
    visual_keys = picked[..., :head_dim]
    visual_vals = picked[..., head_dim:]
    score_visual = (
        jnp.einsum("ctgjd,csgd->cgjts", query_rot, visual_keys, preferred_element_type=jnp.float32)
        * score_scale
    )
    score_text = (
        jnp.einsum("ctgjd,cugd->cgjtu", query_rot, key_text, preferred_element_type=jnp.float32)
        * score_scale
    )
    slots = jnp.arange(cap_length, dtype=jnp.int32)
    causal_mask = slots[None, :] <= slots[:, None]
    score_text = jnp.where(causal_mask, score_text, -jnp.inf)
    top_score = jnp.maximum(jnp.max(score_visual, -1), jnp.max(score_text, -1))[..., None]
    exp_visual = jnp.exp(score_visual - top_score)
    exp_text = jnp.exp(score_text - top_score)
    weight_sum = jnp.sum(exp_visual, -1, keepdims=True) + jnp.sum(exp_text, -1, keepdims=True)
    prob_visual = (exp_visual / weight_sum).astype(jnp.bfloat16)
    prob_text = (exp_text / weight_sum).astype(jnp.bfloat16)
    mixed = jnp.einsum(
        "cgjts,csgd->ctgjd", prob_visual, visual_vals, preferred_element_type=jnp.float32
    )
    mixed = mixed + jnp.einsum(
        "cgjtu,cugd->ctgjd", prob_text, value_text, preferred_element_type=jnp.float32
    )
    valid = slots[None, :] < caption_length[:, None]
    mixed = jnp.where(valid[:, :, None, None, None], mixed, 0.0)
    return mixed.astype(jnp.bfloat16).reshape(row_count, local_heads * head_dim)


def solution(mesh):
    placed = (
        P("dp", None),
        P(),
        P("dp", "mp"),
        P("mp"),
        P("dp", "mp", None),
        P("mp", None),
        P("dp", "mp", None, None),
        P("dp"),
        P("dp"),
        P(),
    )
    return jax.shard_map(
        on_device, mesh=mesh, in_specs=placed, out_specs=P("dp", "mp"), check_vma=False
    )
```

profile of v0, /device:TPU:0, one launch (start us, length us, event | category | flops | bytes accessed | tf_op | source)
XLA Modules:
  0.0 642.6 jit_solution(4969412247455495057)
XLA Ops:
  6.5 0.0 all-gather.8.cloned.1.call-start
  6.5 0.7 all-gather.8.cloned.1.call-update
  7.3 0.0 all-gather.6.cloned.1.call-start
  7.3 0.7 all-gather.6.cloned.1.call-update
  8.0 0.0 all-gather.4.cloned.1.call-start
  8.1 1.1 copy.33
  9.2 15.5 %all_to_all.18 = bf16[1,256,4,256]{3,1,0,2:T(8,128)(2,1)} all-to-all(bf16[1,256,4,256]{3,1,0,2:T(8,128)(2,1)S(1)} %copy.33), channel_id=1, replica_groups=mesh['dp'=32,'mp'=4] {'mp'}, dimensions={2} | all-to-all | bytes 1048576 | tf_op jit(solution)/shard_map/all_to_all | solution.py:47
  24.7 0.0 all-gather.4.cloned.1.call-update
  24.7 0.7 convert_element_type.67
  25.4 0.7 convert_element_type.69
  26.1 0.7 add.92
  26.8 0.9 select_reduce_fusion
  27.7 1.3 iota_compare_fusion.3
  29.0 7.2 %fusion = f32[1024]{0:T(1024)S(1)} fusion(bf16[1024,8192]{1,0:T(8,128)(2,1)} %param.10), kind=kLoop, calls=%fused_computation.2 | loop fusion | flops 25164800 | bytes 16781312 | tf_op jit(solution)/shard_map/reduce_sum | solution.py:43
  36.2 0.2 multiply_cosine_fusion
  36.4 132.0 %all-gather.8.cloned.1.call-done = bf16[8192,1,256]{2,0,1:T(8,128)(2,1)} async-done(((bf16[256,1,256]{2,0,1:T(8,128)(2,1)}), bf16[8192,1,256]{2,0,1:T(8,128)(2,1)}) %all-gather.8.cloned.1.call-update) | async-done | bytes 4194320 | tf_op jit(solution)/shard_map/all_gather | solution.py:64
  168.4 9.6 %fusion.36 = f32[1024,256]{1,0:T(8,128)S(1)} fusion(bf16[8192,1,256]{2,0,1:T(8,128)(2,1)} %all-gather.8.cloned.1.call-done, bf16[1024,8192]{1,0:T(8,128)(2,1)} %param.10, f32[8192]{0:T(1024)S(1)} %convert_element_type.67, f32[1024]{0:T(1024)S(1)} %add_rsqrt_fusion, f32[256]{0:T(256)S(1)} %bitcast.113), kind=kOutput, calls=%fused_computation.45 | convolution fusion | flops 4328783872 | bytes 22057984 | tf_op jit(solution)/shard_map/dot_general | solution.py:61
  178.0 0.0 copy-start.3
  178.0 1.0 copy-done.3
  179.0 0.3 fusion.42
  179.2 184.4 %all-gather.6.cloned.1.call-done = bf16[8192,1024]{1,0:T(8,128)(2,1)} async-done(((bf16[256,1024]{1,0:T(8,128)(2,1)}), bf16[8192,1024]{1,0:T(8,128)(2,1)}) %all-gather.6.cloned.1.call-update) | async-done | bytes 16777232 | tf_op jit(solution)/shard_map/all_gather | solution.py:63
  363.6 22.7 %add_bitcast_fusion = f32[128,8,8,128]{3,1,2,0:T(8,128)S(1)} fusion(bf16[8192,1024]{1,0:T(8,128)(2,1)} %all-gather.6.cloned.1.call-done, bf16[1024,8192]{1,0:T(8,128)(2,1)} %param.10, f32[8192]{0:T(1024)S(1)} %convert_element_type.67, f32[1024]{0:T(1024)S(1)} %add_rsqrt_fusion, f32[1024]{0:T(1024)S(1)} %convert_element_type.69), kind=kOutput, calls=%fused_computation.32 | convolution fusion | flops 17214472192 | bytes 37789696 | tf_op jit(solution)/shard_map/dot_general | solution.py:61
  386.4 1.0 copy.52
  387.4 1.5 fusion.56
  388.9 1.9 fusion.26
  390.8 0.0 copy-start
  390.8 1.3 copy-done
  392.1 4.4 fusion.23
  396.6 160.2 %all-gather.4.cloned.1.call-done = bf16[32,1024,1,256]{3,1,2,0:T(8,128)(2,1)} async-done(((bf16[1,1024,1,256]{3,1,2,0:T(8,128)(2,1)}), bf16[32,1024,1,256]{3,1,2,0:T(8,128)(2,1)}) %all-gather.4.cloned.1.call-update) | async-done | bytes 16777232 | tf_op jit(solution)/shard_map/all_gather | solution.py:52
  556.8 18.5 %convert_bitcast_fusion = bf16[16,1024,1,256]{3,0,1,2:T(8,128)(2,1)} fusion(bf16[32,1024,1,256]{3,1,2,0:T(8,128)(2,1)} %all-gather.4.cloned.1.call-done, s32[16]{0:T(128)S(1)} %select_reduce_fusion), kind=kOutput, calls=%fused_computation.16 | convolution fusion | flops 272630272 | bytes 25165888 | tf_op jit(solution)/shard_map/cn,nsgd->csgd/dot_general | solution.py:55
  575.3 6.1 slice_bitcast_fusion.1
  581.4 17.3 %bitcast_reduce_fusion = (f32[16,8,64]{2,1,0:T(8,128)S(1)}, f32[16,1024,64,8]{1,2,3,0:T(8,128)}) fusion(bf16[16,64,8,64]{3,1,2,0:T(8,128)(2,1)} %copy-done, bf16[16,64,8,64]{3,1,2,0:T(8,128)(2,1)S(1)} %get-tuple-element.5, bf16[16,1024,128,1]{2,0,1,3:T(8,128)(2,1)} %get-tuple-element.8), kind=kOutput, calls=%fused_computation.6 | convolution fusion | flops 2168446976 | bytes 39878656 | tf_op jit(solution)/shard_map/ctgjd,csgd->cgjts/dot_general | solution.py:78
  598.7 0.0 copy-start.1
  598.7 14.5 %fusion.4 = f32[16,8,64]{2,1,0:T(8,128)S(1)} fusion(f32[16,1024,64,8]{1,2,3,0:T(8,128)} %get-tuple-element.16, f32[16,8,64]{2,1,0:T(8,128)S(1)} %max.9), kind=kLoop, calls=%fused_computation.9 | loop fusion | flops 25157632 | bytes 33619968 | tf_op jit(solution)/shard_map/reduce_sum | solution.py:91
  613.2 0.0 copy-start.2
  613.2 0.0 copy-done.1
  613.3 1.4 fusion.22
  614.7 0.7 copy-done.2
  615.4 0.0 copy-start.4
  615.4 0.0 copy-start.5
  615.4 15.0 %fusion.5 = f32[16,128,8,64]{1,3,2,0:T(8,128)S(1)} fusion(f32[16,1024,64,8]{1,2,3,0:T(8,128)} %get-tuple-element.16, f32[16,8,64]{2,1,0:T(8,128)S(1)} %add.89, f32[16,8,64]{2,1,0:T(8,128)S(1)} %max.9, bf16[16,1024,128,1]{2,0,1,3:T(8,128)(2,1)S(1)} %copy-done.2), kind=kOutput, calls=%fused_computation.10 | convolution fusion | flops 2181038080 | bytes 42008576 | tf_op jit(solution)/shard_map/cgjts,csgd->ctgjd/dot_general | solution.py:94
  630.4 0.0 copy-done.4
  630.4 0.0 copy-done.5
  630.4 1.9 fusion.33
  632.4 1.8 copy.40
  634.1 1.9 copy.79
  (6 shorter events, 0.0 us)
Async XLA Ops:
  6.5 161.9 %all-gather.8.cloned.1.call-start = ((), (), s32[]{:S(2)}) async-start(), calls=%async_computation.3 | async-start | bytes 4325376 | tf_op jit(solution)/shard_map/all_gather | solution.py:64
  7.3 356.4 %all-gather.6.cloned.1.call-start = ((), (), s32[]{:S(2)}) async-start(), calls=%async_computation.2 | async-start | bytes 17301504 | tf_op jit(solution)/shard_map/all_gather | solution.py:63
  8.0 548.8 %all-gather.4.cloned.1.call-start = ((), (), s32[]{:S(2)}) async-start(), calls=%async_computation.1 | async-start | bytes 17301504 | tf_op jit(solution)/shard_map/all_gather | solution.py:52
  178.0 1.0 copy-start.3
  390.8 1.3 copy-start
  598.7 14.5 %copy-start.1 = (f32[16,64,64,8]{2,1,3,0:T(8,128)S(1)}, f32[16,64,64,8]{2,1,3,0:T(8,128)}, u32[]{:S(2)}) copy-start(f32[16,64,64,8]{2,1,3,0:T(8,128)} %get-tuple-element.18) | copy-start | bytes 6291460
  613.2 2.2 copy-start.2
  615.4 15.0 %copy-start.4 = (f32[1024,256]{1,0:T(8,128)S(1)}, f32[1024,256]{1,0:T(8,128)}, u32[]{:S(2)}) copy-start(f32[1024,256]{1,0:T(8,128)} %copy-done.3) | copy-start | bytes 3145732
  615.4 15.0 %copy-start.5 = (pred[16,64]{1,0:T(8,128)(4,1)S(1)}, pred[16,64]{1,0:T(8,128)(4,1)}, u32[]{:S(2)}) copy-start(pred[16,64]{1,0:T(8,128)(4,1)} %iota_compare_fusion.3) | copy-start | bytes 3076
Sparse Core Ops, SparseCore 0:
  9.0 159.3 all-gather.7
  170.1 193.5 all-gather.5
  365.3 191.4 all-gather.3
where the time goes:
time: 643 us
  waiting for transfers between devices  478 us (74%)
  matrix products  89.4 us (14%)
  other arithmetic  29.8 us (5%)
  local copies, waits for them, and re-layouts  16.5 us (3%)
  blocking collectives  15.5 us (2%)
  between operations  13.3 us (2%)
    all_gather x1, waiting for transfers between devices, on_device(): lax.all_gather(query_weight, 'dp', axis=0, tiled=True)  184 us
    all_gather x1, waiting for transfers between devices, on_device(): gathered = lax.all_gather(visual, 'dp', axis=0, tiled=True)  160 us
    all_gather x1, waiting for transfers between devices, on_device(): keyval = add_part(lax.all_gather(keyval_weight, 'dp', axis=0, tiled=True))  132 us
    dot_general x2, matrix products, add_part(): return jnp.dot(normed, flat_piece, preferred_element_type=jnp.float32)  32.3 us
    dot_general x1, matrix products, on_device(): jnp.einsum('cn,nsgd->csgd', selector, gathered, preferred_element_type=jn...  18.5 us
    dot_general x1, matrix products, on_device(): jnp.einsum('ctgjd,csgd->cgjts', query_rot, visual_keys, preferred_element...  17.3 us
    all_to_all x1, blocking collectives, on_device(): lax.all_to_all(visual_keyval, 'mp', split_axis=2, concat_axis=1, tiled=True)  15.5 us
    dot_general x1, matrix products, on_device(): jnp.einsum('cgjts,csgd->ctgjd', prob_visual, visual_vals, preferred_eleme...  15 us
  transfers between devices with their start and end apart: 3, of which 3 were waited for; matrix products, arithmetic and copies ran while one was open for 8% of the time, Pallas kernels for 0%

commit v1 on v0

v1 whole, which is shorter than its diff:
```python
import functools
import math

import jax
import jax.numpy as jnp
from jax import lax
from jax.experimental import pallas as pl
from jax.experimental.pallas import tpu as pltpu
from jax.sharding import Mesh
from jax.sharding import PartitionSpec as P

ROPE_BASE = 1000000.0
UNIT = 128
SET_D = (8, 9)
SET_A = (0, 1)
SET_B = (2, 3, 4)
SET_C = (5, 6, 7)
MESH_AXES = ("zl", "x", "y", "zh", "core")
SIZES = {"zl": 2, "x": 4, "y": 4, "zh": 2, "core": 2}
DP = ("zl", "x", "y")
MP = ("zh", "core")
PLANE = ("x", "y")


def shift(value, axis, by):
    size = SIZES[axis]
    return lax.ppermute(value, axis, [(i, (i + by) % size) for i in range(size)])


def norm_body(tokens_ref, gain_ref, out_ref):
    wide = tokens_ref[...].astype(jnp.float32)
    mean_square = jnp.mean(wide * wide, -1, keepdims=True)
    out_ref[...] = (
        wide * lax.rsqrt(mean_square + 1e-06) * gain_ref[...].astype(jnp.float32)
    ).astype(jnp.bfloat16)


def norm_rows(tokens, gain):
    rows, width = tokens.shape
    tile = 128
    return pl.pallas_call(
        norm_body,
        grid=(rows // tile,),
        in_specs=[
            pl.BlockSpec((tile, width), lambda i: (i, 0)),
            pl.BlockSpec((1, width), lambda i: (0, 0)),
        ],
        out_specs=pl.BlockSpec((tile, width), lambda i: (i, 0)),
        out_shape=jax.ShapeDtypeStruct((rows, width), jnp.bfloat16),
        compiler_params=pltpu.CompilerParams(vmem_limit_bytes=40 * 2**20),
        cost_estimate=pl.CostEstimate(
            flops=4 * rows * width, bytes_accessed=4 * rows * width, transcendentals=rows
        ),
        name="norm_rows",
    )(tokens, gain.reshape(1, width))


def project_body(plan, units, has_acc, last, piece, *refs):
    refs = list(refs)
    index_ref = refs.pop(0)
    x_refs = [refs.pop(0) for _ in range(4)]
    count = 1 + max(a for step in plan for a in step)
    w_refs = [refs.pop(0) for _ in range(count)]
    acc_in = refs.pop(0) if has_acc else None
    if last:
        bias_ref, cos_ref, sin_ref = refs.pop(0), refs.pop(0), refs.pop(0)
    out_ref = refs.pop(0)
    w_buf = refs.pop(0)
    acc = refs.pop(0) if last else out_ref
    step = pl.program_id(0)
    steps = len(plan)
    width = w_buf.shape[1]

    seen = {}
    for s, parts in enumerate(plan):
        seen.setdefault(tuple(parts), []).append(s)
    for parts, where in seen.items():
        lo, hi = min(where), max(where)

        @pl.when((step >= lo) & (step <= hi))
        def _(parts=parts):
            at = 0
            for a in parts:
                rows = w_refs[a].shape[0]
                w_buf[pl.ds(at, rows), :] = w_refs[a][...]
                at += rows

    tile = 256

    def add(first):
        def one(i, carry):
            rows = pl.ds(pl.multiple_of(i * tile, tile), tile)
            x = jnp.concatenate([r[rows, :] for r in x_refs], axis=1)
            part = jnp.dot(x, w_buf[...], preferred_element_type=jnp.float32)
            if first:
                if has_acc:
                    acc[rows, :] = acc_in[rows, :] + part
                else:
                    acc[rows, :] = part
            else:
                acc[rows, :] += part
            return carry

        lax.fori_loop(0, x_refs[0].shape[0] // tile, one, 0)

    @pl.when(step == 0)
    def _():
        add(True)

    if steps > 1:

        @pl.when(step > 0)
        def _():
            add(False)

    if last:

        @pl.when(step == steps - 1)
        def _():
            def rope(i, carry):
                rows = pl.ds(pl.multiple_of(i * 64, 64), 64)
                for j, unit in enumerate(units):
                    cols = slice(j * UNIT, (j + 1) * UNIT)
                    value = acc[rows, cols] + bias_ref[:, cols]
                    if unit != 9:
                        value = value * cos_ref[...] + pltpu.roll(value, 64, 1) * sin_ref[...]
                    out_ref[rows, cols] = value.astype(jnp.bfloat16)
                return carry

            lax.fori_loop(0, out_ref.shape[0] // 64, rope, 0)


def project(normed, index, weights, plan, units, acc=None, tail=None):
    rows = normed.shape[0]
    width = weights[0].shape[1]
    steps = len(plan)
    last = tail is not None
    specs = [
        pl.BlockSpec((rows, 256), functools.partial(lambda j, k, idx: (0, idx[4 * k + j]), j))
        for j in range(4)
    ]
    args = [normed] * 4
    for a, w in enumerate(weights):
        uses = [s for s, parts in enumerate(plan) if a in parts]
        if len(uses) == 1:
            specs.append(pl.BlockSpec(w.shape, lambda k, idx: (0, 0)))
        else:
            lo, hi = min(uses), max(uses)
            assert w.shape[0] == 1024 * len(uses)
            specs.append(
                pl.BlockSpec(
                    (1024, width),
                    functools.partial(lambda lo, hi, k, idx: (jnp.clip(k, lo, hi) - lo, 0), lo, hi),
                )
            )
        args.append(w)
    if acc is not None:
        specs.append(pl.BlockSpec((rows, width), lambda k, idx: (0, 0)))
        args.append(acc)
    scratch = [pltpu.VMEM((1024, width), jnp.bfloat16)]
    if last:
        bias, cos, sin = tail
        specs += [
            pl.BlockSpec((1, width), lambda k, idx: (0, 0)),
            pl.BlockSpec(cos.shape, lambda k, idx: (0, 0)),
            pl.BlockSpec(sin.shape, lambda k, idx: (0, 0)),
        ]
        args += [bias, cos, sin]
        scratch.append(pltpu.VMEM((rows, width), jnp.float32))
    kind = jnp.bfloat16 if last else jnp.float32
    return pl.pallas_call(
        functools.partial(project_body, plan, units, acc is not None, last, None),
        grid_spec=pltpu.PrefetchScalarGridSpec(
            num_scalar_prefetch=1,
            grid=(steps,),
            in_specs=specs,
            out_specs=pl.BlockSpec((rows, width), lambda k, idx: (0, 0)),
            scratch_shapes=scratch,
        ),
        out_shape=jax.ShapeDtypeStruct((rows, width), kind),
        compiler_params=pltpu.CompilerParams(vmem_limit_bytes=52 * 2**20),
        cost_estimate=pl.CostEstimate(
            flops=2 * rows * 1024 * steps * width,
            bytes_accessed=steps * 2 * 1024 * (rows + width) + rows * width * 4,
            transcendentals=0,
        ),
        name="project",
    )(index, *args)


def attend_body(counts, length, which_ref, len_ref, *refs):
    refs = list(refs)
    q_refs = [refs.pop(0) for _ in counts]
    text_ref, visual_ref, out_ref = refs
    now = pl.program_id(0)
    used = len_ref[now]
    head_dim = UNIT
    factor = 1.0 / math.sqrt(head_dim) * math.log2(math.e)
    nt = (((1,), (1,)), ((), ()))

    def run(rows):
        parts = []
        for ref, count in zip(q_refs, counts):
            parts += [ref[0:rows, j * UNIT : (j + 1) * UNIT] for j in range(count)]
        query = jnp.concatenate(parts, axis=0)
        heads = len(parts)
        visual = visual_ref[...].reshape(-1, 2 * head_dim)
        text = text_ref[...]
        sv = lax.dot_general(
            query, visual[:, :head_dim], nt, preferred_element_type=jnp.float32
        )
        st = lax.dot_general(query, text[:, :head_dim], nt, preferred_element_type=jnp.float32)
        at = lax.broadcasted_iota(jnp.int32, st.shape, 0) % rows
        st = jnp.where(lax.broadcasted_iota(jnp.int32, st.shape, 1) <= at, st, -jnp.inf)
        top = jnp.maximum(
            jnp.max(sv, -1, keepdims=True), jnp.max(st, -1, keepdims=True)
        )
        ev = jnp.exp2((sv - top) * factor)
        et = jnp.exp2((st - top) * factor)
        total = jnp.sum(ev, -1, keepdims=True) + jnp.sum(et, -1, keepdims=True)
        inverse = 1.0 / total
        pv = (ev * inverse).astype(jnp.bfloat16)
        pt = (et * inverse).astype(jnp.bfloat16)
        mixed = jnp.dot(pv, visual[:, head_dim:], preferred_element_type=jnp.float32)
        mixed += jnp.dot(pt, text[:, head_dim:], preferred_element_type=jnp.float32)
        keep = lax.broadcasted_iota(jnp.int32, (rows, head_dim), 0) < used
        for h in range(heads):
            out_ref[0:rows, h * UNIT : (h + 1) * UNIT] = jnp.where(
                keep, mixed[h * rows : (h + 1) * rows], 0.0
            ).astype(jnp.bfloat16)
        if rows < length:
            out_ref[rows:length, :] = jnp.zeros((length - rows, out_ref.shape[1]), jnp.bfloat16)

    tiles = length // 16
    for tile in range(1, tiles + 1):

        @pl.when((used > 16 * (tile - 1)) & (used <= 16 * tile))
        def _(tile=tile):
            run(16 * tile)


def attend(which, lengths, queries, text, visual):
    captions = which.shape[0]
    rows = queries[0].shape[0]
    length = rows // captions
    counts = tuple(q.shape[1] // UNIT for q in queries)
    width = sum(counts) * UNIT
    relays, _, chunk, depth = visual.shape
    return pl.pallas_call(
        functools.partial(attend_body, counts, length),
        grid_spec=pltpu.PrefetchScalarGridSpec(
            num_scalar_prefetch=2,
            grid=(captions,),
            in_specs=[
                pl.BlockSpec((length, q.shape[1]), lambda c, which, lens: (c, 0)) for q in queries
            ]
            + [
                pl.BlockSpec((length, text.shape[1]), lambda c, which, lens: (c, 0)),
                pl.BlockSpec(
                    (relays, 1, chunk, depth), lambda c, which, lens: (0, which[c], 0, 0)
                ),
            ],
            out_specs=pl.BlockSpec((length, width), lambda c, which, lens: (c, 0)),
        ),
        out_shape=jax.ShapeDtypeStruct((rows, width), jnp.bfloat16),
        compiler_params=pltpu.CompilerParams(vmem_limit_bytes=52 * 2**20),
        cost_estimate=pl.CostEstimate(
            flops=4 * rows * width * relays * chunk,
            bytes_accessed=4 * rows * width,
            transcendentals=rows * (width // UNIT) * relays * chunk,
        ),
        name="attend",
    )(which, lengths, *queries, text, visual)


def ring_gather(unit, axis):
    half = unit.shape[0] // 2
    before = shift(unit, axis, 1)
    after = shift(unit, axis, -1)
    far_head = shift(before[:half], axis, 1)
    far_tail = shift(after[half:], axis, -1)
    return before, after, far_head, far_tail


def line_gather(piece, axis):
    return jnp.concatenate(
        [piece, shift(piece, axis, 1), shift(piece, axis, -1), shift(piece, axis, 2)], axis=0
    )


def on_device(
    tokens,
    norm_gain,
    query_weight,
    query_bias,
    keyval_weight,
    keyval_bias,
    visual_keyval,
    caption_image,
    caption_length,
    image_owner,
):
    zl, x, y = (lax.axis_index(a) for a in DP)
    here = lax.axis_index(DP)
    rows = tokens.shape[0]
    depth = query_weight.shape[0]
    head_dim = keyval_weight.shape[2] // 2
    weight = jnp.concatenate([query_weight, keyval_weight.reshape(depth, -1)], axis=1)
    bias = jnp.concatenate([query_bias, keyval_bias.reshape(-1)]).astype(jnp.float32)[None]

    def pick(array, units):
        return jnp.concatenate([array[:, u * UNIT : (u + 1) * UNIT] for u in units], axis=1)

    w_d, w_a, w_b, w_c = (pick(weight, s) for s in (SET_D, SET_A, SET_B, SET_C))

    a_other = shift(w_a, "zl", 1)
    d_own = lax.all_gather(w_d, PLANE, axis=0, tiled=True)
    line_b = line_gather(w_b, "y")
    line_c = line_gather(w_c, "x")
    cross_b = shift(line_b, "zl", 1)
    cross_c = shift(line_c, "zl", 1)
    d_cross = shift(d_own, "zl", 1)
    both = jnp.where(zl == 0, jnp.concatenate([w_a, a_other]), jnp.concatenate([a_other, w_a]))
    a_full = lax.all_gather(both, PLANE, axis=0, tiled=True)
    own_b = ring_gather(line_b, "x")
    own_c = ring_gather(line_c, "y")
    far_b = ring_gather(cross_b, "x")
    far_c = ring_gather(cross_c, "y")

    tok_local = visual_keyval.shape[1]
    kv_heads = visual_keyval.shape[2]
    images = image_owner.shape[0]
    chunk = tok_local // images
    spread = visual_keyval.reshape(images, chunk, kv_heads, 2 * head_dim).transpose(0, 2, 1, 3)
    spread = spread.reshape(images * kv_heads, chunk, 2 * head_dim)
    held = lax.all_to_all(spread, DP + MP, split_axis=0, concat_axis=0, tiled=True)
    held = held.reshape(images, kv_heads * chunk, 2 * head_dim)
    target = jnp.arange(images, dtype=jnp.int32)
    wanted = jnp.stack([image_owner[jnp.maximum(target - 1, 0)], image_owner[target]], axis=1)
    selector = (wanted[:, :, None] == target[None, None, :]).astype(jnp.bfloat16)
    sent = jnp.einsum(
        "isn,ntd->istd", selector, held, preferred_element_type=jnp.float32
    ).astype(jnp.bfloat16)
    visual = lax.all_to_all(sent, DP, split_axis=0, concat_axis=0, tiled=True)
    which = jnp.clip(caption_image - here + 1, 0, 1).astype(jnp.int32)

    half = head_dim // 2
    length = rows // caption_image.shape[0]
    vis_tokens = tok_local * kv_heads
    freqs = ROPE_BASE ** (-jnp.arange(half, dtype=jnp.float32) / half)
    positions = (vis_tokens + jnp.arange(length, dtype=jnp.int32)).astype(jnp.float32)
    angles = positions[:, None] * freqs[None, :]
    cos = jnp.concatenate([jnp.cos(angles)] * 2, axis=1)
    sin = jnp.concatenate([-jnp.sin(angles), jnp.sin(angles)], axis=1)

    def tail(units):
        return pick(bias, units), cos, sin

    normed = norm_rows(tokens, norm_gain)
    line = jnp.arange(4, dtype=jnp.int32)
    turn = jnp.array([0, -1, 1, 2], jnp.int32)

    def line_index_b(plane, at_x):
        return plane * 16 + at_x % 4 * 4 + (y + turn) % 4

    def line_index_c(plane, at_y):
        return plane * 16 + (x + turn) % 4 * 4 + at_y % 4

    other = 1 - zl

    def ring_project(units, line_of, at, line_arr, own, cross_arr, cross):
        before, after, head, tail_half = own
        fbefore, fafter, fhead, ftail = cross
        acc = project(
            normed,
            jnp.concatenate([line_of(zl, at), line_of(zl, at - 1), line_of(zl, at + 1)]),
            [line_arr, before, after],
            [(0,), (1,), (2,)],
            units,
        )
        acc = project(
            normed,
            jnp.concatenate(
                [line_of(zl, at + 2), line_of(other, at), line_of(other, at - 1), line_of(other, at + 1)]
            ),
            [head, tail_half, cross_arr, fbefore, fafter],
            [(0, 1), (2,), (3,), (4,)],
            units,
            acc,
        )
        return project(
            normed, line_of(other, at + 2), [fhead, ftail], [(0, 1)], units, acc, tail(units)
        )

    span = jnp.arange(16, dtype=jnp.int32)
    acc_d = project(normed, zl * 16 + span, [d_own], [(0,)] * 4, SET_D)
    q_b = ring_project(SET_B, line_index_b, x, line_b, own_b, cross_b, far_b)
    q_c = ring_project(SET_C, line_index_c, y, line_c, own_c, cross_c, far_c)
    text = project(normed, other * 16 + span, [d_cross], [(0,)] * 4, SET_D, acc_d, tail(SET_D))
    order_a = jnp.stack([span, span + 16], axis=1).reshape(-1)
    q_a = project(normed, order_a, [a_full], [(0,)] * 8, SET_A, None, tail(SET_A))
    return attend(which, caption_length, [q_a, q_b, q_c], text, visual)


def solution(mesh):
    grid = Mesh(mesh.devices.reshape(tuple(SIZES[a] for a in MESH_AXES)), MESH_AXES)
    placed = (
        P(DP, None),
        P(),
        P(DP, MP),
        P(MP),
        P(DP, MP, None),
        P(MP, None),
        P(DP, MP, None, None),
        P(DP),
        P(DP),
        P(),
    )
    return jax.shard_map(
        on_device, mesh=grid, in_specs=placed, out_specs=P(DP, MP), check_vma=False
    )
```

time: 643 us -> 272 us (0.42)
  waiting for transfers between devices: 478 us -> 50.1 us
  Pallas kernels: 0 us -> 125 us
  matrix products: 89.4 us -> 1.55 us
  starting transfers between devices: 0.08 us -> 62.1 us
  other arithmetic: 29.8 us -> 1.69 us
  blocking collectives: 15.5 us -> 0 us
    all_gather x3 -> x2, waiting for transfers between devices: 477 us -> 0.02 us  [the longest x1 0.02 us: on_device(): a_full = lax.all_gather(both, PLANE, axis=0, tiled=True)]
    pallas_call x0 -> x11, Pallas kernels: none -> 125 us  [the longest x9 87.9 us: project(): pl.pallas_call(functools.partial(project_body, plan, units, acc is not No...]
    dot_general x7 -> x1, matrix products: 89.4 us -> 1.55 us  [on_device(): jnp.einsum('isn,ntd->istd', selector, held, preferred_element_type=jnp.fl...]
    ppermute x0 -> x26, waiting for transfers between devices: none -> 49.3 us  [shift(): lax.ppermute(value, axis, [(i, (i + by) % size) for i in range(size)])]
    ppermute x0 -> x26, starting transfers between devices: none -> 45.3 us  [shift(): lax.ppermute(value, axis, [(i, (i + by) % size) for i in range(size)])]
    reduce_sum x4 -> x0, other arithmetic: 24 us -> none  [the longest x1 14.5 us: on_device(): jnp.sum(exp_visual, -1, keepdims=True)]
    all_to_all x0 -> x2, starting transfers between devices: none -> 16.9 us  [the longest x1 8.9 us: on_device(): lax.all_to_all(spread, DP + MP, split_axis=0, concat_axis=0, tiled=True)]
    all_to_all x1 -> x0, blocking collectives: 15.5 us -> none  [on_device(): lax.all_to_all(visual_keyval, 'mp', split_axis=2, concat_axis=1, tiled=True)]
  transfers between devices with their start and end apart: 3 -> 30, of which waited for: 3 -> 6; matrix products, arithmetic and copies ran while one was open for 8% -> 6% of each run, Pallas kernels for 0% -> 39%
where the time goes in v1:
time: 272 us; the launch traced here: 267 us
  Pallas kernels  125 us (46%)
  starting transfers between devices  62.1 us (23%)
  waiting for transfers between devices  50.1 us (18%)
  between operations  14 us (5%)
  local copies, waits for them, and re-layouts  12.4 us (5%)
    pallas_call x9, Pallas kernels, project(): pl.pallas_call(functools.partial(project_body, plan, units, acc is not No...  87.9 us
    ppermute x26, waiting for transfers between devices, shift(): lax.ppermute(value, axis, [(i, (i + by) % size) for i in range(size)])  49.3 us
    ppermute x26, starting transfers between devices, shift(): lax.ppermute(value, axis, [(i, (i + by) % size) for i in range(size)])  45.3 us
    pallas_call x1, Pallas kernels, attend(): pl.pallas_call(functools.partial(attend_body, counts, length), grid_spec=...  20.2 us
    pallas_call x1, Pallas kernels, norm_rows(): pl.pallas_call(norm_body, grid=(rows // tile,), in_specs=[pl.BlockSpec((t...  17.2 us
    all_to_all x1, starting transfers between devices, on_device(): lax.all_to_all(spread, DP + MP, split_axis=0, concat_axis=0, tiled=True)  8.9 us
    all_to_all x1, starting transfers between devices, on_device(): visual = lax.all_to_all(sent, DP, split_axis=0, concat_axis=0, tiled=True)  7.96 us
  transfers between devices with their start and end apart: 30, of which 6 were waited for; matrix products, arithmetic and copies ran while one was open for 6% of the time, Pallas kernels for 39%

profile of v1, /device:TPU:0, one launch (start us, length us, event | category | flops | bytes accessed | tf_op | source)
XLA Modules:
  0.0 267.2 jit_solution(8495428686605085962)
XLA Ops:
  6.5 0.7 all-gather.6.cloned.1.call-update
  7.3 0.9 concatenate.58
  8.2 2.1 collective-permute-start
  10.3 3.5 %collective-permute-done = bf16[256,256]{1,0:T(8,128)(2,1)S(1)} collective-permute-done((bf16[256,256]{1,0:T(8,128)(2,1)S(1)}, bf16[256,256]{1,0:T(8,128)(2,1)S(1)}, u32[]{:S(2)}, u32[]{:S(2)}) %collective-permute-start) | collective-permute-done | bytes 131104 | tf_op jit(solution)/shard_map/ppermute | solution.py:27
  13.8 0.8 maximum_select_fusion
  14.7 1.1 fusion.12
  15.7 1.6 collective-permute-start.13
  17.3 1.7 collective-permute-start.14
  19.0 1.8 collective-permute-start.15
  20.8 1.6 collective-permute-start.1
  22.4 1.7 collective-permute-start.2
  24.2 0.9 copy.21
  25.0 8.9 %all-to-all-start = ((bf16[128,8,256]{2,1,0:T(8,128)(2,1)}), bf16[128,8,256]{2,1,0:T(8,128)(2,1)}, u32[]{:S(2)}, u32[]{:S(2)}) async-start(bf16[128,8,256]{2,1,0:T(8,128)(2,1)} %bitcast.8), calls=%async_computation | async-start | bytes 1048576 | tf_op jit(solution)/shard_map/all_to_all | solution.py:336
  34.2 0.1 copy.19
  34.2 0.1 reshape.75.refs_0_
  34.4 0.7 gather_fusion
  35.1 0.7 gather_fusion.1
  35.8 17.2 %norm_rows.1.refs_1_.refs_2_.refs_3_.refs_4_ = bf16[1024,8192]{1,0:T(8,128)(2,1)} custom-call(bf16[1024,8192]{1,0:T(8,128)(2,1)} %tokens_ref.1, bf16[1,8192]{1,0:T(2,128)(2,1)S(1)} %reshape.76.gain_ref), custom_call_target="tpu_custom_call" | custom-call | flops 33554432 | bytes 33554432 | tf_op jit(solution)/shard_map/norm_rows/pallas_call | solution.py:41
  53.2 2.5 collective-permute-start.3
  55.8 0.7 collective-permute-start.21
  56.5 2.7 %collective-permute-start.23 = (bf16[1024,384]{1,0:T(8,128)(2,1)S(1)}, bf16[1024,384]{1,0:T(8,128)(2,1)S(1)}, u32[]{:S(2)}, u32[]{:S(2)}) collective-permute-start(bf16[1024,384]{1,0:T(8,128)(2,1)S(1)} %pad_maximum_fusion.1.refs_5_), channel_id=1, source_target_pairs={{0,12},{4,0},{8,4},{12,8},{1,13},{5,1},{9,5},{13,9},{2,14},{6,2},{... | collective-permute-start | bytes 2359304 | tf_op jit(solution)/shard_map/ppermute | solution.py:27
  59.2 1.6 collective-permute-start.16
  60.8 1.7 collective-permute-done.3
  62.7 2.1 collective-permute-start.11
  64.8 1.6 collective-permute-start.4
  66.4 14.6 %collective-permute-done.21.refs_6_ = bf16[1024,384]{1,0:T(8,128)(2,1)S(1)} collective-permute-done((bf16[1024,384]{1,0:T(8,128)(2,1)S(1)}, bf16[1024,384]{1,0:T(8,128)(2,1)S(1)}, u32[]{:S(2)}, u32[]{:S(2)}) %collective-permute-start.21) | collective-permute-done | bytes 786464 | tf_op jit(solution)/shard_map/ppermute | solution.py:27
  81.1 2.0 collective-permute-start.9
  83.2 0.2 fusion.6
  83.4 2.2 collective-permute-start.17
  85.6 1.1 collective-permute-start.19
  86.7 8.2 %collective-permute-done.4.refs_7_ = bf16[1024,384]{1,0:T(8,128)(2,1)} collective-permute-done((bf16[1024,384]{1,0:T(8,128)(2,1)S(1)}, bf16[1024,384]{1,0:T(8,128)(2,1)}, u32[]{:S(2)}, u32[]{:S(2)}) %collective-permute-start.4) | collective-permute-done | bytes 786464 | tf_op jit(solution)/shard_map/ppermute | solution.py:27
  94.9 1.5 collective-permute-start.5
  96.4 1.8 collective-permute-start.7
  98.2 12.5 %collective-permute-done.9.refs_6_ = bf16[1024,384]{1,0:T(8,128)(2,1)S(1)} collective-permute-done((bf16[1024,384]{1,0:T(8,128)(2,1)S(1)}, bf16[1024,384]{1,0:T(8,128)(2,1)S(1)}, u32[]{:S(2)}, u32[]{:S(2)}) %collective-permute-start.9) | collective-permute-done | bytes 786464 | tf_op jit(solution)/shard_map/ppermute | solution.py:27
  110.7 1.7 collective-permute-start.25
  112.5 0.1 pad_maximum_fusion.2
  112.6 1.5 fusion
  114.1 1.6 copy.31
  115.7 8.0 %all-to-all-start.1 = ((bf16[32,2,32,256]{3,2,1,0:T(8,128)(2,1)}), bf16[32,2,32,256]{3,2,1,0:T(8,128)(2,1)}, u32[]{:S(2)}, u32[]{:S(2)}) async-start(bf16[32,2,32,256]{3,2,1,0:T(8,128)(2,1)} %copy.31), calls=%async_computation.1 | async-start | bytes 2097152 | tf_op jit(solution)/shard_map/all_to_all | solution.py:344
  123.7 1.1 slice.83
  125.0 2.0 collective-permute-start.22
  126.9 1.5 collective-permute-start.24
  128.5 8.8 %collective-permute-done.5.refs_8_ = bf16[1024,384]{1,0:T(8,128)(2,1)} collective-permute-done((bf16[1024,384]{1,0:T(8,128)(2,1)}, bf16[1024,384]{1,0:T(8,128)(2,1)}, u32[]{:S(2)}, u32[]{:S(2)}) %collective-permute-start.5) | collective-permute-done | bytes 786464 | tf_op jit(solution)/shard_map/ppermute | solution.py:27
  137.3 1.2 collective-permute-start.10
  138.4 2.1 collective-permute-start.12
  140.5 9.3 %project.13.refs_10_ = f32[1024,384]{1,0:T(8,128)} custom-call(s32[12]{0:T(128)S(1)} %pad_add_fusion.5.refs_0_, bf16[1024,8192]{1,0:T(8,128)(2,1)} %norm_rows.1.refs_1_.refs_2_.refs_3_.refs_4_, bf16[1024,8192]{1,0:T(8,128)(2,1)} %norm_rows.1.refs_1_.refs_2_.refs_3_.refs_4_, bf16[1024,8192]{1,0:T(8,128)(2,1)} %norm_rows.1.refs_1_.refs_2_.refs_3_.refs_4_, ...), custom_call_target="tpu_custom_call" | custom-call | flops 2415919104 | bytes 10223616 | tf_op jit(solution)/shard_map/project/pallas_call | solution.py:171
  149.8 9.3 %project.10.refs_10_ = f32[1024,384]{1,0:T(8,128)} custom-call(s32[12]{0:T(128)S(1)} %pad_add_fusion.3.refs_0_, bf16[1024,8192]{1,0:T(8,128)(2,1)} %norm_rows.1.refs_1_.refs_2_.refs_3_.refs_4_, bf16[1024,8192]{1,0:T(8,128)(2,1)} %norm_rows.1.refs_1_.refs_2_.refs_3_.refs_4_, bf16[1024,8192]{1,0:T(8,128)(2,1)} %norm_rows.1.refs_1_.refs_2_.refs_3_.refs_4_, ...), custom_call_target="tpu_custom_call" | custom-call | flops 2415919104 | bytes 10223616 | tf_op jit(solution)/shard_map/project/pallas_call | solution.py:171
  159.1 1.0 slice.80
  160.1 1.0 slice.81
  161.2 1.0 slice.76
  162.2 1.0 slice.77
  163.3 2.4 collective-permute-start.18
  165.7 0.9 collective-permute-start.20
  166.6 0.6 collective-permute-start.6
  167.2 2.6 collective-permute-start.8
  169.8 12.3 %project.14.refs_7_ = f32[1024,384]{1,0:T(8,128)} custom-call(s32[16]{0:T(128)S(1)} %pad_add_fusion.4.refs_0_, bf16[1024,8192]{1,0:T(8,128)(2,1)} %norm_rows.1.refs_1_.refs_2_.refs_3_.refs_4_, bf16[1024,8192]{1,0:T(8,128)(2,1)} %norm_rows.1.refs_1_.refs_2_.refs_3_.refs_4_, bf16[1024,8192]{1,0:T(8,128)(2,1)} %norm_rows.1.refs_1_.refs_2_.refs_3_.refs_4_, ...), custom_call_target="tpu_custom_call" | custom-call | flops 3221225472 | bytes 13107200 | tf_op jit(solution)/shard_map/project/pallas_call | solution.py:171
  182.1 12.2 %project.11.refs_7_ = f32[1024,384]{1,0:T(8,128)} custom-call(s32[16]{0:T(128)S(1)} %pad_add_fusion.2.refs_0_, bf16[1024,8192]{1,0:T(8,128)(2,1)} %norm_rows.1.refs_1_.refs_2_.refs_3_.refs_4_, bf16[1024,8192]{1,0:T(8,128)(2,1)} %norm_rows.1.refs_1_.refs_2_.refs_3_.refs_4_, bf16[1024,8192]{1,0:T(8,128)(2,1)} %norm_rows.1.refs_1_.refs_2_.refs_3_.refs_4_, ...), custom_call_target="tpu_custom_call" | custom-call | flops 3221225472 | bytes 13107200 | tf_op jit(solution)/shard_map/project/pallas_call | solution.py:171
  194.3 6.0 %project.15.refs_2_ = bf16[1024,384]{1,0:T(8,128)(2,1)S(1)} custom-call(s32[4]{0:T(128)S(1)} %get-tuple-element.26.refs_0_, bf16[1024,8192]{1,0:T(8,128)(2,1)} %norm_rows.1.refs_1_.refs_2_.refs_3_.refs_4_, bf16[1024,8192]{1,0:T(8,128)(2,1)} %norm_rows.1.refs_1_.refs_2_.refs_3_.refs_4_, bf16[1024,8192]{1,0:T(8,128)(2,1)} %norm_rows.1.refs_1_.refs_2_.refs_3_.refs_4_, ...), custom_call_target="tpu_custom_call" | custom-call | flops 805306368 | bytes 4456448 | tf_op jit(solution)/shard_map/project/pallas_call | solution.py:171
  200.3 0.9 copy-done.2
  201.2 6.0 %project.12.refs_1_ = bf16[1024,384]{1,0:T(8,128)(2,1)S(1)} custom-call(s32[4]{0:T(128)S(1)} %get-tuple-element.35.refs_0_, bf16[1024,8192]{1,0:T(8,128)(2,1)} %norm_rows.1.refs_1_.refs_2_.refs_3_.refs_4_, bf16[1024,8192]{1,0:T(8,128)(2,1)} %norm_rows.1.refs_1_.refs_2_.refs_3_.refs_4_, bf16[1024,8192]{1,0:T(8,128)(2,1)} %norm_rows.1.refs_1_.refs_2_.refs_3_.refs_4_, ...), custom_call_target="tpu_custom_call" | custom-call | flops 805306368 | bytes 4456448 | tf_op jit(solution)/shard_map/project/pallas_call | solution.py:171
  207.2 8.0 %project.16.refs_6_ = f32[1024,256]{1,0:T(8,128)S(1)} custom-call(s32[16]{0:T(128)S(1)} %iota_add_fusion.refs_0_, bf16[1024,8192]{1,0:T(8,128)(2,1)} %norm_rows.1.refs_1_.refs_2_.refs_3_.refs_4_, bf16[1024,8192]{1,0:T(8,128)(2,1)} %norm_rows.1.refs_1_.refs_2_.refs_3_.refs_4_, bf16[1024,8192]{1,0:T(8,128)(2,1)} %norm_rows.1.refs_1_.refs_2_.refs_3_.refs_4_, ...), custom_call_target="tpu_custom_call" | custom-call | flops 2147483648 | bytes 11534336 | tf_op jit(solution)/shard_map/project/pallas_call | solution.py:171
  215.2 9.3 %project.17.refs_3_ = bf16[1024,256]{1,0:T(8,128)(2,1)S(1)} custom-call(s32[16]{0:T(128)S(1)} %iota_add_fusion.1.refs_0_, bf16[1024,8192]{1,0:T(8,128)(2,1)} %norm_rows.1.refs_1_.refs_2_.refs_3_.refs_4_, bf16[1024,8192]{1,0:T(8,128)(2,1)} %norm_rows.1.refs_1_.refs_2_.refs_3_.refs_4_, bf16[1024,8192]{1,0:T(8,128)(2,1)} %norm_rows.1.refs_1_.refs_2_.refs_3_.refs_4_, ...), custom_call_target="tpu_custom_call" | custom-call | flops 2147483648 | bytes 11534336 | tf_op jit(solution)/shard_map/project/pallas_call | solution.py:171
  224.6 15.5 %project.9.refs_0_ = bf16[1024,256]{1,0:T(8,128)(2,1)S(1)} custom-call(s32[32]{0:T(128)S(1)} %reshape.75.refs_0_, bf16[1024,8192]{1,0:T(8,128)(2,1)} %norm_rows.1.refs_1_.refs_2_.refs_3_.refs_4_, bf16[1024,8192]{1,0:T(8,128)(2,1)} %norm_rows.1.refs_1_.refs_2_.refs_3_.refs_4_, bf16[1024,8192]{1,0:T(8,128)(2,1)} %norm_rows.1.refs_1_.refs_2_.refs_3_.refs_4_, ...), custom_call_target="tpu_custom_call" | custom-call | flops 4294967296 | bytes 22020096 | tf_op jit(solution)/shard_map/project/pallas_call | solution.py:171
  240.1 20.2 %attend.1 = bf16[1024,1024]{1,0:T(8,128)(2,1)} custom-call(s32[16]{0:T(128)S(1)} %add_clamp_fusion.which_ref, s32[16]{0:T(128)S(1)} %copy-done.3, bf16[1024,256]{1,0:T(8,128)(2,1)S(1)} %project.9.refs_0_, bf16[1024,384]{1,0:T(8,128)(2,1)S(1)} %project.12.refs_1_, bf16[1024,384]{1,0:T(8,128)(2,1)} %copy-done.2, bf16[1024,256]{1,0:T(8,128)(2,1)S(1)} %project.17.refs_3_, ...), custom_call_target="tpu_custom_call" | custom-call | flops 4294967296 | bytes 4194304 | tf_op jit(solution)/shard_map/attend/pallas_call | solution.py:249
  (83 shorter events, 1.0 us)
Async XLA Ops:
  6.5 27.8 %copy-start = (s32[32]{0:T(128)S(1)}, s32[32]{0:T(128)}, u32[]{:S(2)}) copy-start(s32[32]{0:T(128)} %param.20) | copy-start | bytes 388
  6.5 17.6 %copy-start.7 = (bf16[1,256,4,256]{3,2,1,0:T(4,128)(2,1)S(1)}, bf16[1,256,4,256]{3,2,1,0:T(4,128)(2,1)}, u32[]{:S(2)}) copy-start(bf16[1,256,4,256]{3,2,1,0:T(4,128)(2,1)} %param.17) | copy-start | bytes 1572868
  6.5 104.1 %all-gather.6.cloned.1.call-start = ((), (), s32[]{:S(2)}) async-start(), calls=%async_computation.3 | async-start | bytes 2228224 | tf_op jit(solution)/shard_map/all_gather | solution.py:317
  7.3 217.3 %all-gather.4.cloned.1.call-start = ((), (), s32[]{:S(2)}) async-start(), calls=%async_computation.2 | async-start | bytes 4456448 | tf_op jit(solution)/shard_map/all_gather | solution.py:324
  8.2 5.6 %collective-permute-start = (bf16[256,256]{1,0:T(8,128)(2,1)S(1)}, bf16[256,256]{1,0:T(8,128)(2,1)S(1)}, u32[]{:S(2)}, u32[]{:S(2)}) collective-permute-start(bf16[256,256]{1,0:T(8,128)(2,1)S(1)} %concatenate.58), channel_id=1, source_target_pairs={{0,64},{64,0},{1,65},{65,1},{2,66},{66,2},{3,67},{67,3},{4,68},{68... | collective-permute-start | bytes 393224 | tf_op jit(solution)/shard_map/ppermute | solution.py:27
  15.7 37.4 %collective-permute-start.13 = (bf16[256,384]{1,0:T(8,128)(2,1)S(1)}, bf16[256,384]{1,0:T(8,128)(2,1)S(1)}, u32[]{:S(2)}, u32[]{:S(2)}) collective-permute-start(bf16[256,384]{1,0:T(8,128)(2,1)S(1)} %get-tuple-element.12), channel_id=1, source_target_pairs={{0,16},{16,32},{32,48},{48,0},{1,17},{17,33},{33,49},{49,1},{2,18}... | collective-permute-start | bytes 589832 | tf_op jit(solution)/shard_map/ppermute | solution.py:27
  17.3 38.4 %collective-permute-start.14 = (bf16[256,384]{1,0:T(8,128)(2,1)S(1)}, bf16[256,384]{1,0:T(8,128)(2,1)S(1)}, u32[]{:S(2)}, u32[]{:S(2)}) collective-permute-start(bf16[256,384]{1,0:T(8,128)(2,1)S(1)} %get-tuple-element.12), channel_id=1, source_target_pairs={{0,48},{16,0},{32,16},{48,32},{1,49},{17,1},{33,17},{49,33},{2,50}... | collective-permute-start | bytes 589832 | tf_op jit(solution)/shard_map/ppermute | solution.py:27
  19.0 36.7 %collective-permute-start.15 = (bf16[256,384]{1,0:T(8,128)(2,1)S(1)}, bf16[256,384]{1,0:T(8,128)(2,1)S(1)}, u32[]{:S(2)}, u32[]{:S(2)}) collective-permute-start(bf16[256,384]{1,0:T(8,128)(2,1)S(1)} %get-tuple-element.12), channel_id=1, source_target_pairs={{0,32},{16,48},{32,0},{48,16},{1,33},{17,49},{33,1},{49,17},{2,34}... | collective-permute-start | bytes 589832 | tf_op jit(solution)/shard_map/ppermute | solution.py:27
  20.8 13.2 %copy-start.8 = (bf16[8192]{0:T(1024)(128)(2,1)S(1)}, bf16[8192]{0:T(1024)(128)(2,1)}, u32[]{:S(2)}) copy-start(bf16[8192]{0:T(1024)(128)(2,1)} %param.12) | copy-start | bytes 49156
  20.8 13.2 %copy-start.10 = (bf16[1024]{0:T(1024)(128)(2,1)S(1)}, bf16[1024]{0:T(1024)(128)(2,1)}, u32[]{:S(2)}) copy-start(bf16[1024]{0:T(1024)(128)(2,1)} %param.14) | copy-start | bytes 6148
  20.8 38.3 %collective-permute-start.1 = (bf16[256,384]{1,0:T(8,128)(2,1)S(1)}, bf16[256,384]{1,0:T(8,128)(2,1)S(1)}, u32[]{:S(2)}, u32[]{:S(2)}) collective-permute-start(bf16[256,384]{1,0:T(8,128)(2,1)S(1)} %get-tuple-element.13), channel_id=1, source_target_pairs={{0,4},{4,8},{8,12},{12,0},{1,5},{5,9},{9,13},{13,1},{2,6},{6,10},{... | collective-permute-start | bytes 589832 | tf_op jit(solution)/shard_map/ppermute | solution.py:27
  22.4 38.4 %collective-permute-start.2 = (bf16[256,384]{1,0:T(8,128)(2,1)S(1)}, bf16[256,384]{1,0:T(8,128)(2,1)S(1)}, u32[]{:S(2)}, u32[]{:S(2)}) collective-permute-start(bf16[256,384]{1,0:T(8,128)(2,1)S(1)} %get-tuple-element.13), channel_id=1, source_target_pairs={{0,12},{4,0},{8,4},{12,8},{1,13},{5,1},{9,5},{13,9},{2,14},{6,2},{... | collective-permute-start | bytes 589832 | tf_op jit(solution)/shard_map/ppermute | solution.py:27
  25.0 87.5 %all-to-all-start = ((bf16[128,8,256]{2,1,0:T(8,128)(2,1)}), bf16[128,8,256]{2,1,0:T(8,128)(2,1)}, u32[]{:S(2)}, u32[]{:S(2)}) async-start(bf16[128,8,256]{2,1,0:T(8,128)(2,1)} %bitcast.8), calls=%async_computation | async-start | bytes 1048576 | tf_op jit(solution)/shard_map/all_to_all | solution.py:336
  35.8 17.3 %copy-start.9 = (bf16[1,256]{1,0:T(2,128)(2,1)S(1)}, bf16[1,256]{1,0:T(2,128)(2,1)}, u32[]{:S(2)}) copy-start(bf16[1,256]{1,0:T(2,128)(2,1)} %param.16) | copy-start | bytes 1540
  35.8 17.3 %copy-start.11 = (s32[4]{0:T(128)S(1)}, s32[4]{0:T(128)}, u32[]{:S(2)}) copy-start(s32[4]{0:T(128)} %constant.155.clone) | copy-start | bytes 52
  53.1 59.4 %copy-start.12 = (s32[16]{0:T(128)S(1)}, s32[16]{0:T(128)}, u32[]{:S(2)}) copy-start(s32[16]{0:T(128)} %param.18) | copy-start | bytes 196
  53.2 9.4 %collective-permute-start.3 = (bf16[256,384]{1,0:T(8,128)(2,1)S(1)}, bf16[256,384]{1,0:T(8,128)(2,1)S(1)}, u32[]{:S(2)}, u32[]{:S(2)}) collective-permute-start(bf16[256,384]{1,0:T(8,128)(2,1)S(1)} %get-tuple-element.13), channel_id=1, source_target_pairs={{0,8},{4,12},{8,0},{12,4},{1,9},{5,13},{9,1},{13,5},{2,10},{6,14},... | collective-permute-start | bytes 589832 | tf_op jit(solution)/shard_map/ppermute | solution.py:27
  55.8 25.3 %collective-permute-start.21 = (bf16[1024,384]{1,0:T(8,128)(2,1)S(1)}, bf16[1024,384]{1,0:T(8,128)(2,1)S(1)}, u32[]{:S(2)}, u32[]{:S(2)}) collective-permute-start(bf16[1024,384]{1,0:T(8,128)(2,1)S(1)} %pad_maximum_fusion.1.refs_5_), channel_id=1, source_target_pairs={{0,4},{4,8},{8,12},{12,0},{1,5},{5,9},{9,13},{13,1},{2,6},{6,10},{... | collective-permute-start | bytes 2359304 | tf_op jit(solution)/shard_map/ppermute | solution.py:27
  56.5 29.1 %collective-permute-start.23 = (bf16[1024,384]{1,0:T(8,128)(2,1)S(1)}, bf16[1024,384]{1,0:T(8,128)(2,1)S(1)}, u32[]{:S(2)}, u32[]{:S(2)}) collective-permute-start(bf16[1024,384]{1,0:T(8,128)(2,1)S(1)} %pad_maximum_fusion.1.refs_5_), channel_id=1, source_target_pairs={{0,12},{4,0},{8,4},{12,8},{1,13},{5,1},{9,5},{13,9},{2,14},{6,2},{... | collective-permute-start | bytes 2359304 | tf_op jit(solution)/shard_map/ppermute | solution.py:27
  59.2 24.2 %collective-permute-start.16 = (bf16[1024,384]{1,0:T(8,128)(2,1)S(1)}, bf16[1024,384]{1,0:T(8,128)(2,1)}, u32[]{:S(2)}, u32[]{:S(2)}) collective-permute-start(bf16[1024,384]{1,0:T(8,128)(2,1)S(1)} %pad_maximum_fusion.1.refs_5_), channel_id=1, source_target_pairs={{0,64},{64,0},{1,65},{65,1},{2,66},{66,2},{3,67},{67,3},{4,68},{68... | collective-permute-start | bytes 2359304 | tf_op jit(solution)/shard_map/ppermute | solution.py:27
  62.7 33.7 %collective-permute-start.11 = (bf16[1024,384]{1,0:T(8,128)(2,1)S(1)}, bf16[1024,384]{1,0:T(8,128)(2,1)S(1)}, u32[]{:S(2)}, u32[]{:S(2)}) collective-permute-start(bf16[1024,384]{1,0:T(8,128)(2,1)S(1)} %pad_maximum_fusion.refs_5_), channel_id=1, source_target_pairs={{0,48},{16,0},{32,16},{48,32},{1,49},{17,1},{33,17},{49,33},{2,50}... | collective-permute-start | bytes 2359304 | tf_op jit(solution)/shard_map/ppermute | solution.py:27
  64.8 30.1 %collective-permute-start.4 = (bf16[1024,384]{1,0:T(8,128)(2,1)S(1)}, bf16[1024,384]{1,0:T(8,128)(2,1)}, u32[]{:S(2)}, u32[]{:S(2)}) collective-permute-start(bf16[1024,384]{1,0:T(8,128)(2,1)S(1)} %pad_maximum_fusion.refs_5_), channel_id=1, source_target_pairs={{0,64},{64,0},{1,65},{65,1},{2,66},{66,2},{3,67},{67,3},{4,68},{68... | collective-permute-start | bytes 2359304 | tf_op jit(solution)/shard_map/ppermute | solution.py:27
  81.1 29.6 %collective-permute-start.9 = (bf16[1024,384]{1,0:T(8,128)(2,1)S(1)}, bf16[1024,384]{1,0:T(8,128)(2,1)S(1)}, u32[]{:S(2)}, u32[]{:S(2)}) collective-permute-start(bf16[1024,384]{1,0:T(8,128)(2,1)S(1)} %pad_maximum_fusion.refs_5_), channel_id=1, source_target_pairs={{0,16},{16,32},{32,48},{48,0},{1,17},{17,33},{33,49},{49,1},{2,18}... | collective-permute-start | bytes 2359304 | tf_op jit(solution)/shard_map/ppermute | solution.py:27
  83.4 41.5 %collective-permute-start.17 = (bf16[1024,384]{1,0:T(8,128)(2,1)}, bf16[1024,384]{1,0:T(8,128)(2,1)}, u32[]{:S(2)}, u32[]{:S(2)}) collective-permute-start(bf16[1024,384]{1,0:T(8,128)(2,1)} %collective-permute-done.16.refs_7_), channel_id=1, source_target_pairs={{0,4},{4,8},{8,12},{12,0},{1,5},{5,9},{9,13},{13,1},{2,6},{6,10},{... | collective-permute-start | bytes 2359304 | tf_op jit(solution)/shard_map/ppermute | solution.py:27
  85.6 12.6 %copy-start.4 = (bf16[1024,384]{1,0:T(8,128)(2,1)}, bf16[1024,384]{1,0:T(8,128)(2,1)S(1)}, u32[]{:S(2)}) copy-start(bf16[1024,384]{1,0:T(8,128)(2,1)S(1)} %collective-permute-done.23.refs_7_) | copy-start | bytes 2359300
  85.6 41.3 %collective-permute-start.19 = (bf16[1024,384]{1,0:T(8,128)(2,1)}, bf16[1024,384]{1,0:T(8,128)(2,1)}, u32[]{:S(2)}, u32[]{:S(2)}) collective-permute-start(bf16[1024,384]{1,0:T(8,128)(2,1)} %collective-permute-done.16.refs_7_), channel_id=1, source_target_pairs={{0,12},{4,0},{8,4},{12,8},{1,13},{5,1},{9,5},{13,9},{2,14},{6,2},{... | collective-permute-start | bytes 2359304 | tf_op jit(solution)/shard_map/ppermute | solution.py:27
  94.9 42.4 %collective-permute-start.5 = (bf16[1024,384]{1,0:T(8,128)(2,1)}, bf16[1024,384]{1,0:T(8,128)(2,1)}, u32[]{:S(2)}, u32[]{:S(2)}) collective-permute-start(bf16[1024,384]{1,0:T(8,128)(2,1)} %collective-permute-done.4.refs_7_), channel_id=1, source_target_pairs={{0,16},{16,32},{32,48},{48,0},{1,17},{17,33},{33,49},{49,1},{2,18}... | collective-permute-start | bytes 2359304 | tf_op jit(solution)/shard_map/ppermute | solution.py:27
  96.4 1.9 copy-start.5
  96.4 42.0 %collective-permute-start.7 = (bf16[1024,384]{1,0:T(8,128)(2,1)}, bf16[1024,384]{1,0:T(8,128)(2,1)}, u32[]{:S(2)}, u32[]{:S(2)}) collective-permute-start(bf16[1024,384]{1,0:T(8,128)(2,1)} %collective-permute-done.4.refs_7_), channel_id=1, source_target_pairs={{0,48},{16,0},{32,16},{48,32},{1,49},{17,1},{33,17},{49,33},{2,50}... | collective-permute-start | bytes 2359304 | tf_op jit(solution)/shard_map/ppermute | solution.py:27
  110.7 104.5 %collective-permute-start.25 = (bf16[4096,256]{1,0:T(8,128)(2,1)}, bf16[4096,256]{1,0:T(8,128)(2,1)}, u32[]{:S(2)}, u32[]{:S(2)}) collective-permute-start(bf16[4096,256]{1,0:T(8,128)(2,1)} %bitcast.21), channel_id=1, source_target_pairs={{0,64},{64,0},{1,65},{65,1},{2,66},{66,2},{3,67},{67,3},{4,68},{68... | collective-permute-start | bytes 6291464 | tf_op jit(solution)/shard_map/ppermute | solution.py:27
  115.7 124.4 %all-to-all-start.1 = ((bf16[32,2,32,256]{3,2,1,0:T(8,128)(2,1)}), bf16[32,2,32,256]{3,2,1,0:T(8,128)(2,1)}, u32[]{:S(2)}, u32[]{:S(2)}) async-start(bf16[32,2,32,256]{3,2,1,0:T(8,128)(2,1)} %copy.31), calls=%async_computation.1 | async-start | bytes 2097152 | tf_op jit(solution)/shard_map/all_to_all | solution.py:344
  123.7 1.3 copy-start.6
  125.0 38.3 %collective-permute-start.22 = (bf16[512,384]{1,0:T(8,128)(2,1)S(1)}, bf16[512,384]{1,0:T(8,128)(2,1)S(1)}, u32[]{:S(2)}, u32[]{:S(2)}) collective-permute-start(bf16[512,384]{1,0:T(8,128)(2,1)S(1)} %slice.82), channel_id=1, source_target_pairs={{0,4},{4,8},{8,12},{12,0},{1,5},{5,9},{9,13},{13,1},{2,6},{6,10},{... | collective-permute-start | bytes 1179656 | tf_op jit(solution)/shard_map/ppermute | solution.py:27
  126.9 38.7 %collective-permute-start.24 = (bf16[512,384]{1,0:T(8,128)(2,1)S(1)}, bf16[512,384]{1,0:T(8,128)(2,1)S(1)}, u32[]{:S(2)}, u32[]{:S(2)}) collective-permute-start(bf16[512,384]{1,0:T(8,128)(2,1)S(1)} %slice.83), channel_id=1, source_target_pairs={{0,12},{4,0},{8,4},{12,8},{1,13},{5,1},{9,5},{13,9},{2,14},{6,2},{... | collective-permute-start | bytes 1179656 | tf_op jit(solution)/shard_map/ppermute | solution.py:27
  137.3 29.3 %collective-permute-start.10 = (bf16[512,384]{1,0:T(8,128)(2,1)S(1)}, bf16[512,384]{1,0:T(8,128)(2,1)S(1)}, u32[]{:S(2)}, u32[]{:S(2)}) collective-permute-start(bf16[512,384]{1,0:T(8,128)(2,1)S(1)} %slice.78), channel_id=1, source_target_pairs={{0,16},{16,32},{32,48},{48,0},{1,17},{17,33},{33,49},{49,1},{2,18}... | collective-permute-start | bytes 1179656 | tf_op jit(solution)/shard_map/ppermute | solution.py:27
  138.4 28.7 %collective-permute-start.12 = (bf16[512,384]{1,0:T(8,128)(2,1)S(1)}, bf16[512,384]{1,0:T(8,128)(2,1)S(1)}, u32[]{:S(2)}, u32[]{:S(2)}) collective-permute-start(bf16[512,384]{1,0:T(8,128)(2,1)S(1)} %slice.79), channel_id=1, source_target_pairs={{0,48},{16,0},{32,16},{48,32},{1,49},{17,1},{33,17},{49,33},{2,50}... | collective-permute-start | bytes 1179656 | tf_op jit(solution)/shard_map/ppermute | solution.py:27
  163.3 31.1 %collective-permute-start.18 = (bf16[512,384]{1,0:T(8,128)(2,1)S(1)}, bf16[512,384]{1,0:T(8,128)(2,1)S(1)}, u32[]{:S(2)}, u32[]{:S(2)}) collective-permute-start(bf16[512,384]{1,0:T(8,128)(2,1)S(1)} %slice.80), channel_id=1, source_target_pairs={{0,4},{4,8},{8,12},{12,0},{1,5},{5,9},{9,13},{13,1},{2,6},{6,10},{... | collective-permute-start | bytes 1179656 | tf_op jit(solution)/shard_map/ppermute | solution.py:27
  165.7 28.6 %collective-permute-start.20 = (bf16[512,384]{1,0:T(8,128)(2,1)S(1)}, bf16[512,384]{1,0:T(8,128)(2,1)S(1)}, u32[]{:S(2)}, u32[]{:S(2)}) collective-permute-start(bf16[512,384]{1,0:T(8,128)(2,1)S(1)} %slice.81), channel_id=1, source_target_pairs={{0,12},{4,0},{8,4},{12,8},{1,13},{5,1},{9,5},{13,9},{2,14},{6,2},{... | collective-permute-start | bytes 1179656 | tf_op jit(solution)/shard_map/ppermute | solution.py:27
  166.6 34.6 %collective-permute-start.6 = (bf16[512,384]{1,0:T(8,128)(2,1)S(1)}, bf16[512,384]{1,0:T(8,128)(2,1)S(1)}, u32[]{:S(2)}, u32[]{:S(2)}) collective-permute-start(bf16[512,384]{1,0:T(8,128)(2,1)S(1)} %slice.76), channel_id=1, source_target_pairs={{0,16},{16,32},{32,48},{48,0},{1,17},{17,33},{33,49},{49,1},{2,18}... | collective-permute-start | bytes 1179656 | tf_op jit(solution)/shard_map/ppermute | solution.py:27
  167.2 34.0 %collective-permute-start.8 = (bf16[512,384]{1,0:T(8,128)(2,1)S(1)}, bf16[512,384]{1,0:T(8,128)(2,1)S(1)}, u32[]{:S(2)}, u32[]{:S(2)}) collective-permute-start(bf16[512,384]{1,0:T(8,128)(2,1)S(1)} %slice.77), channel_id=1, source_target_pairs={{0,48},{16,0},{32,16},{48,32},{1,49},{17,1},{33,17},{49,33},{2,50}... | collective-permute-start | bytes 1179656 | tf_op jit(solution)/shard_map/ppermute | solution.py:27
  200.3 0.9 copy-start.2
  224.6 15.6 %copy-start.3 = (s32[16]{0:T(128)S(1)}, s32[16]{0:T(128)}, u32[]{:S(2)}) copy-start(s32[16]{0:T(128)} %len_ref.1) | copy-start | bytes 196
  240.1 20.2 %copy-start.1 = (s32[32]{0:T(128)S(1)}, s32[32]{0:T(128)}, u32[]{:S(2)}) copy-start(s32[32]{0:T(128)} %param.20) | copy-start | bytes 388
Sparse Core Ops, SparseCore 0:
  9.5 47.6 all-gather.5
  59.3 69.7 all-gather.3

commit v2 on v1

v2 whole, which is shorter than its diff:
```python
import functools
import math

import jax
import jax.numpy as jnp
from jax import lax
from jax.experimental import pallas as pl
from jax.experimental.pallas import tpu as pltpu
from jax.sharding import Mesh
from jax.sharding import PartitionSpec as P

ROPE_BASE = 1000000.0
UNIT = 128
PIECE = 256
STEP = 1024
SET_D = (8, 9)
SET_B = (0, 1, 2, 3)
SET_C = (4, 5, 6, 7)
MESH_AXES = ("zl", "x", "y", "zh", "core")
SIZES = {"zl": 2, "x": 4, "y": 4, "zh": 2, "core": 2}
DP = ("zl", "x", "y")
MP = ("zh", "core")
PLANE = ("x", "y")
MIB = 2**20


def shift(value, axis, by):
    size = SIZES[axis]
    return lax.ppermute(value, axis, [(i, (i + by) % size) for i in range(size)])


def whole():
    return pl.BlockSpec(memory_space=pltpu.VMEM)


def norm_body(tokens_ref, gain_ref, out_ref, buf, sems):
    rows = tokens_ref.shape[0]
    depth, tile = buf.shape[:2]
    count = rows // tile

    def copy(i, slot):
        at = pl.multiple_of(i * tile, tile)
        return pltpu.make_async_copy(tokens_ref.at[pl.ds(at, tile)], buf.at[slot], sems.at[slot])

    for i in range(depth - 1):
        copy(i, i).start()
    gain = gain_ref[...].astype(jnp.float32)

    def one(i, carry):
        slot = lax.rem(i, depth)

        @pl.when(i + depth - 1 < count)
        def _():
            copy(i + depth - 1, lax.rem(i + depth - 1, depth)).start()

        copy(i, slot).wait()
        for part in range(tile // 16):
            wide = buf[slot, part * 16 : (part + 1) * 16, :].astype(jnp.float32)
            mean_square = jnp.mean(wide * wide, -1, keepdims=True)
            out_ref[pl.ds(pl.multiple_of(i * tile + part * 16, 16), 16), :] = (
                wide * lax.rsqrt(mean_square + 1e-06) * gain
            ).astype(jnp.bfloat16)
        return carry

    lax.fori_loop(0, count, one, 0)


def norm_rows(tokens, gain):
    rows, width = tokens.shape
    depth, tile = 4, 64
    return pl.pallas_call(
        norm_body,
        in_specs=[pl.BlockSpec(memory_space=pl.ANY), whole()],
        out_specs=whole(),
        out_shape=jax.ShapeDtypeStruct((rows, width), jnp.bfloat16),
        scratch_shapes=[
            pltpu.VMEM((depth, tile, width), jnp.bfloat16),
            pltpu.SemaphoreType.DMA((depth,)),
        ],
        compiler_params=pltpu.CompilerParams(vmem_limit_bytes=24 * MIB),
        cost_estimate=pl.CostEstimate(
            flops=4 * rows * width, bytes_accessed=4 * rows * width, transcendentals=rows
        ),
        name="norm_rows",
    )(tokens, gain.reshape(1, width))


def project_body(rows_of, has_acc, units, index_ref, x_ref, *refs):
    refs = list(refs)
    w_refs = [refs.pop(0) for _ in rows_of]
    acc_in = refs.pop(0) if has_acc else None
    if units:
        bias_ref, cos_ref, sin_ref = refs.pop(0), refs.pop(0), refs.pop(0)
    out_ref, w_buf, sems = refs.pop(0), refs.pop(0), refs.pop(0)
    acc = refs.pop(0) if units else out_ref
    steps = sum(rows_of) // STEP

    copies = [[] for _ in range(steps)]
    at = 0
    for ref, count in zip(w_refs, rows_of):
        done = 0
        while done < count:
            s, into = divmod(at, STEP)
            size = min(count - done, STEP - into)
            copies[s].append(
                pltpu.make_async_copy(
                    ref.at[pl.ds(done, size)],
                    w_buf.at[pl.ds(at, size)],
                    sems.at[s, len(copies[s])],
                )
            )
            done += size
            at += size
    for group in copies:
        for copy in group:
            copy.start()

    tile = 256
    for s in range(steps):
        for copy in copies[s]:
            copy.wait()
        w = w_buf.at[pl.ds(s * STEP, STEP)]
        cols = [
            pl.ds(pl.multiple_of(index_ref[4 * s + j] * PIECE, PIECE), PIECE) for j in range(4)
        ]
        for m in range(0, x_ref.shape[0], tile):
            x = jnp.concatenate([x_ref[m : m + tile, c] for c in cols], axis=1)
            part = jnp.dot(x, w[...], preferred_element_type=jnp.float32)
            if s > 0:
                part += acc[m : m + tile, :]
            elif has_acc:
                part += acc_in[m : m + tile, :]
            acc[m : m + tile, :] = part

    if units:

        def rope(i, carry):
            rows = pl.ds(pl.multiple_of(i * 64, 64), 64)
            for j, unit in enumerate(units):
                cols = slice(j * UNIT, (j + 1) * UNIT)
                value = acc[rows, cols] + bias_ref[:, cols]
                if unit != 9:
                    value = value * cos_ref[...] + pltpu.roll(value, 64, 1) * sin_ref[...]
                out_ref[rows, cols] = value.astype(jnp.bfloat16)
            return carry

        lax.fori_loop(0, out_ref.shape[0] // 64, rope, 0)


def project(normed, index, weights, acc=None, units=None, tail=()):
    rows = normed.shape[0]
    width = weights[0].shape[1]
    rows_of = [w.shape[0] for w in weights]
    total = sum(rows_of)
    scratch = [
        pltpu.VMEM((total, width), jnp.bfloat16),
        pltpu.SemaphoreType.DMA((total // STEP, 4)),
    ]
    if units:
        scratch.append(pltpu.VMEM((rows, width), jnp.float32))
    accs = [] if acc is None else [acc]
    return pl.pallas_call(
        functools.partial(project_body, rows_of, acc is not None, units),
        in_specs=[pl.BlockSpec(memory_space=pltpu.SMEM), whole()]
        + [pl.BlockSpec(memory_space=pl.ANY)] * len(weights)
        + [whole()] * (len(accs) + len(tail)),
        out_specs=whole(),
        out_shape=jax.ShapeDtypeStruct((rows, width), jnp.bfloat16 if units else jnp.float32),
        scratch_shapes=scratch,
        compiler_params=pltpu.CompilerParams(vmem_limit_bytes=30 * MIB),
        cost_estimate=pl.CostEstimate(
            flops=2 * rows * total * width, bytes_accessed=2 * total * width, transcendentals=0
        ),
        name="project",
    )(index, normed, *weights, *accs, *tail)


def attend_body(length, has_before, which_ref, len_ref, q_ref, text_ref, visual_ref, *refs):
    out_ref = refs[-1]
    now = pl.program_id(0)
    used = len_ref[now]
    heads = q_ref.shape[1] // UNIT
    factor = 1.0 / math.sqrt(UNIT) * math.log2(math.e)
    nt = (((1,), (1,)), ((), ()))

    def run(rows):
        query = jnp.concatenate(
            [q_ref[0:rows, j * UNIT : (j + 1) * UNIT] for j in range(heads)], axis=0
        )
        visual = visual_ref[...].reshape(-1, 2 * UNIT)
        text = text_ref[...]
        sv = lax.dot_general(query, visual[:, :UNIT], nt, preferred_element_type=jnp.float32)
        st = lax.dot_general(query, text[:, :UNIT], nt, preferred_element_type=jnp.float32)
        at = lax.broadcasted_iota(jnp.int32, st.shape, 0) % rows
        st = jnp.where(lax.broadcasted_iota(jnp.int32, st.shape, 1) <= at, st, -jnp.inf)
        top = jnp.maximum(jnp.max(sv, -1, keepdims=True), jnp.max(st, -1, keepdims=True))
        ev = jnp.exp2((sv - top) * factor)
        et = jnp.exp2((st - top) * factor)
        inverse = 1.0 / (jnp.sum(ev, -1, keepdims=True) + jnp.sum(et, -1, keepdims=True))
        pv = (ev * inverse).astype(jnp.bfloat16)
        pt = (et * inverse).astype(jnp.bfloat16)
        mixed = jnp.dot(pv, visual[:, UNIT:], preferred_element_type=jnp.float32)
        mixed += jnp.dot(pt, text[:, UNIT:], preferred_element_type=jnp.float32)
        keep = lax.broadcasted_iota(jnp.int32, (rows, UNIT), 0) < used
        for h in range(heads):
            out_ref[0:rows, h * UNIT : (h + 1) * UNIT] = jnp.where(
                keep, mixed[h * rows : (h + 1) * rows], 0.0
            ).astype(jnp.bfloat16)
        if rows < length:
            out_ref[rows:length, :] = jnp.zeros((length - rows, out_ref.shape[1]), jnp.bfloat16)

    for tile in range(1, length // 16 + 1):

        @pl.when((used > 16 * (tile - 1)) & (used <= 16 * tile))
        def _(tile=tile):
            run(16 * tile)


def attend(which, lengths, query, text, visual, place, out_width, before=None):
    captions = which.shape[0]
    rows, width = query.shape
    length = rows // captions
    relays, _, chunk, depth = visual.shape
    befores = [] if before is None else [before]
    return pl.pallas_call(
        functools.partial(attend_body, length, before is not None),
        grid_spec=pltpu.PrefetchScalarGridSpec(
            num_scalar_prefetch=2,
            grid=(captions,),
            in_specs=[
                pl.BlockSpec((length, width), lambda c, which, lens: (c, 0)),
                pl.BlockSpec((length, text.shape[1]), lambda c, which, lens: (c, 0)),
                pl.BlockSpec(
                    (relays, 1, chunk, depth), lambda c, which, lens: (0, which[c], 0, 0)
                ),
            ]
            + [pl.BlockSpec(memory_space=pl.ANY)] * len(befores),
            out_specs=pl.BlockSpec((length, width), lambda c, which, lens: (c, place)),
        ),
        out_shape=jax.ShapeDtypeStruct((rows, out_width), jnp.bfloat16),
        input_output_aliases={5: 0} if befores else {},
        compiler_params=pltpu.CompilerParams(vmem_limit_bytes=24 * MIB),
        cost_estimate=pl.CostEstimate(
            flops=4 * rows * width * relays * chunk,
            bytes_accessed=4 * rows * width,
            transcendentals=rows * (width // UNIT) * relays * chunk,
        ),
        name="attend",
    )(which, lengths, query, text, visual, *befores)


def line_gather(piece, axis):
    return jnp.concatenate(
        [piece, shift(piece, axis, 1), shift(piece, axis, -1), shift(piece, axis, 2)], axis=0
    )


def on_device(
    tokens,
    norm_gain,
    query_weight,
    query_bias,
    keyval_weight,
    keyval_bias,
    visual_keyval,
    caption_image,
    caption_length,
    image_owner,
):
    zl, x, y = (lax.axis_index(a) for a in DP)
    here = lax.axis_index(DP)
    rows = tokens.shape[0]
    depth = query_weight.shape[0]
    head_dim = keyval_weight.shape[2] // 2
    weight = jnp.concatenate([query_weight, keyval_weight.reshape(depth, -1)], axis=1)
    bias = jnp.concatenate([query_bias, keyval_bias.reshape(-1)]).astype(jnp.float32)[None]

    def pick(array, units):
        return array[:, units[0] * UNIT : (units[-1] + 1) * UNIT]

    w_d, w_b, w_c = (pick(weight, s) for s in (SET_D, SET_B, SET_C))

    d_own = lax.all_gather(w_d, PLANE, axis=0, tiled=True)
    line_b = line_gather(w_b, "y")
    line_c = line_gather(w_c, "x")
    cross_b = shift(line_b, "zl", 1)
    cross_c = shift(line_c, "zl", 1)
    d_cross = shift(d_own, "zl", 1)

    def big(line, cross, axis):
        own_before, own_after = shift(line, axis, 1), shift(line, axis, -1)
        own_far = shift(own_before, axis, 1)
        cross_before, cross_after = shift(cross, axis, 1), shift(cross, axis, -1)
        cross_far = shift(cross_after, axis, -1)
        return [line, own_before, own_after], [own_far, cross, cross_before, cross_after], cross_far

    parts_b = big(line_b, cross_b, "x")
    parts_c = big(line_c, cross_c, "y")

    tok_local = visual_keyval.shape[1]
    kv_heads = visual_keyval.shape[2]
    images = image_owner.shape[0]
    chunk = tok_local // images
    spread = visual_keyval.reshape(images, chunk, kv_heads, 2 * head_dim).transpose(0, 2, 1, 3)
    spread = spread.reshape(images * kv_heads, chunk, 2 * head_dim)
    held = lax.all_to_all(spread, DP + MP, split_axis=0, concat_axis=0, tiled=True)
    held = held.reshape(images, kv_heads * chunk, 2 * head_dim)
    target = jnp.arange(images, dtype=jnp.int32)
    wanted = jnp.stack([image_owner[jnp.maximum(target - 1, 0)], image_owner[target]], axis=1)
    selector = (wanted[:, :, None] == target[None, None, :]).astype(jnp.bfloat16)
    sent = jnp.einsum(
        "isn,ntd->istd", selector, held, preferred_element_type=jnp.float32
    ).astype(jnp.bfloat16)
    visual = lax.all_to_all(sent, DP, split_axis=0, concat_axis=0, tiled=True)
    which = jnp.clip(caption_image - here + 1, 0, 1).astype(jnp.int32)

    half = head_dim // 2
    length = rows // caption_image.shape[0]
    vis_tokens = tok_local * kv_heads
    freqs = ROPE_BASE ** (-jnp.arange(half, dtype=jnp.float32) / half)
    positions = (vis_tokens + jnp.arange(length, dtype=jnp.int32)).astype(jnp.float32)
    angles = positions[:, None] * freqs[None, :]
    cos = jnp.concatenate([jnp.cos(angles)] * 2, axis=1)
    sin = jnp.concatenate([-jnp.sin(angles), jnp.sin(angles)], axis=1)

    def tail(units):
        return pick(bias, units), cos, sin

    normed = norm_rows(tokens, norm_gain)
    turn = jnp.array([0, -1, 1, 2], jnp.int32)
    other = 1 - zl

    def line_of_b(plane, by):
        return plane * 16 + (x + by) % 4 * 4 + (y + turn) % 4

    def line_of_c(plane, by):
        return plane * 16 + (x + turn) % 4 * 4 + (y + by) % 4

    def ring_project(units, line_of, parts):
        early, later, final = parts
        acc = project(
            normed, jnp.concatenate([line_of(zl, 0), line_of(zl, -1), line_of(zl, 1)]), early
        )
        acc = project(
            normed,
            jnp.concatenate(
                [line_of(zl, 2), line_of(other, 0), line_of(other, -1), line_of(other, 1)]
            ),
            later,
            acc,
        )
        return project(normed, line_of(other, 2), [final], acc, units, tail(units))

    span = jnp.arange(16, dtype=jnp.int32)
    acc_d = project(normed, zl * 16 + span, [d_own])
    text = project(normed, other * 16 + span, [d_cross], acc_d, SET_D, tail(SET_D))
    q_b = ring_project(SET_B, line_of_b, parts_b)
    width = query_weight.shape[1]
    out = attend(which, caption_length, q_b, text, visual, 0, width)
    q_c = ring_project(SET_C, line_of_c, parts_c)
    return attend(which, caption_length, q_c, text, visual, 1, width, out)


def solution(mesh):
    grid = Mesh(mesh.devices.reshape(tuple(SIZES[a] for a in MESH_AXES)), MESH_AXES)
    placed = (
        P(DP, None),
        P(),
        P(DP, MP),
        P(MP),
        P(DP, MP, None),
        P(MP, None),
        P(DP, MP, None, None),
        P(DP),
        P(DP),
        P(),
    )
    return jax.shard_map(
        on_device, mesh=grid, in_specs=placed, out_specs=P(DP, MP), check_vma=False
    )
```

time: 272 us -> 254 us (0.934); the launches traced: 267 us -> 253 us
  Pallas kernels: 125 us -> 89.7 us
  waiting for transfers between devices: 50.1 us -> 70.9 us
  local copies, waits for them, and re-layouts: 12.4 us -> 26.9 us
  starting transfers between devices: 62.1 us -> 47.7 us
    pallas_call x11, Pallas kernels: 125 us -> 89.7 us  [the longest x8 49.2 us: project(): pl.pallas_call(functools.partial(project_body, rows_of, acc is not None,...]
    unnamed x27 -> x37, local copies, waits for them, and re-layouts: 1.04 us -> 21.9 us
    ppermute x26 -> x21, waiting for transfers between devices: 49.3 us -> 70.2 us  [shift(): lax.ppermute(value, axis, [(i, (i + by) % size) for i in range(size)])]
    ppermute x26 -> x21, starting transfers between devices: 45.3 us -> 31.5 us  [shift(): lax.ppermute(value, axis, [(i, (i + by) % size) for i in range(size)])]
    slice x9 -> x2, local copies, waits for them, and re-layouts: 6.44 us -> 1.07 us  [pick(): return array[:, units[0] * UNIT:(units[-1] + 1) * UNIT]]
  transfers between devices with their start and end apart: 30 -> 24, of which waited for: 6 -> 3; matrix products, arithmetic and copies ran while one was open for 6% -> 4% of each run, Pallas kernels for 39% -> 24%
where the time goes in v2:
time: 254 us; the launch traced here: 253 us
  Pallas kernels  89.7 us (35%)
  waiting for transfers between devices  70.9 us (28%)
  starting transfers between devices  47.7 us (19%)
  local copies, waits for them, and re-layouts  26.9 us (11%)
  between operations  13.9 us (5%)
    ppermute x21, waiting for transfers between devices, shift(): lax.ppermute(value, axis, [(i, (i + by) % size) for i in range(size)])  70.2 us
    pallas_call x8, Pallas kernels, project(): pl.pallas_call(functools.partial(project_body, rows_of, acc is not None,...  49.2 us
    ppermute x21, starting transfers between devices, shift(): lax.ppermute(value, axis, [(i, (i + by) % size) for i in range(size)])  31.5 us
    pallas_call x2, Pallas kernels, attend(): pl.pallas_call(functools.partial(attend_body, length, before is not None)...  29.1 us
    unnamed x37, local copies, waits for them, and re-layouts  21.9 us
    pallas_call x1, Pallas kernels, norm_rows(): pl.pallas_call(norm_body, in_specs=[pl.BlockSpec(memory_space=pl.ANY), wh...  11.3 us
    all_to_all x1, starting transfers between devices, on_device(): lax.all_to_all(spread, DP + MP, split_axis=0, concat_axis=0, tiled=True)  8.73 us
    all_to_all x1, starting transfers between devices, on_device(): visual = lax.all_to_all(sent, DP, split_axis=0, concat_axis=0, tiled=True)  7.42 us
  transfers between devices with their start and end apart: 24, of which 3 were waited for; matrix products, arithmetic and copies ran while one was open for 4% of the time, Pallas kernels for 24%

profile of v2, /device:TPU:0, one launch (start us, length us, event | category | flops | bytes accessed | tf_op | source)
XLA Modules:
  0.0 252.5 jit_solution(6972982086070555083)
XLA Ops:
  6.5 0.7 all-gather.3.cloned.1.call-update
  7.3 1.1 fusion.11
  8.3 1.7 collective-permute-start.11
  10.1 1.6 collective-permute-start.12
  11.6 2.1 collective-permute-start.13
  13.7 1.5 collective-permute-start
  15.2 1.7 collective-permute-start.1
  17.0 1.1 copy.28
  18.1 0.9 copy.17
  18.9 8.7 %all-to-all-start = ((bf16[128,8,256]{2,1,0:T(8,128)(2,1)}), bf16[128,8,256]{2,1,0:T(8,128)(2,1)}, u32[]{:S(2)}, u32[]{:S(2)}) async-start(bf16[128,8,256]{2,1,0:T(8,128)(2,1)} %bitcast.8), calls=%async_computation | async-start | bytes 1048576 | tf_op jit(solution)/shard_map/all_to_all | solution.py:306
  27.7 0.7 gather_fusion
  28.5 0.7 gather_fusion.1
  29.3 0.0 copy-start.13
  29.3 0.1 pad_maximum_fusion.1.refs_0_
  29.4 1.0 collective-permute-start.17
  30.4 2.4 collective-permute-start.20
  32.7 1.0 collective-permute-start.14
  33.7 1.9 collective-permute-start.2
  35.6 0.0 copy-start.12
  35.7 0.7 copy-done.12
  36.3 37.1 %collective-permute-done.2 = bf16[256,512]{1,0:T(8,128)(2,1)} collective-permute-done((bf16[256,512]{1,0:T(8,128)(2,1)S(1)}, bf16[256,512]{1,0:T(8,128)(2,1)}, u32[]{:S(2)}, u32[]{:S(2)}) %collective-permute-start.2) | collective-permute-done | bytes 262176 | tf_op jit(solution)/shard_map/ppermute | solution.py:29
  73.4 1.2 pad_maximum_fusion.refs_0_
  74.6 1.2 collective-permute-start.6
  75.8 1.6 collective-permute-start.3
  77.4 2.2 collective-permute-start.9
  79.6 0.1 pad_add_fusion.4.index_ref
  79.7 1.2 collective-permute-start.15
  80.8 0.8 collective-permute-start.19
  81.7 0.1 pad_add_fusion.2.index_ref
  81.8 0.2 fusion.6
  82.0 19.1 %collective-permute-done.6.refs_1_ = bf16[1024,512]{1,0:T(8,128)(2,1)} collective-permute-done((bf16[1024,512]{1,0:T(8,128)(2,1)S(1)}, bf16[1024,512]{1,0:T(8,128)(2,1)}, u32[]{:S(2)}, u32[]{:S(2)}) %collective-permute-start.6) | collective-permute-done | bytes 1048608 | tf_op jit(solution)/shard_map/ppermute | solution.py:29
  101.0 0.6 collective-permute-start.18
  101.6 1.2 collective-permute-start.4
  102.8 0.1 pad_add_fusion.3.index_ref
  102.9 0.1 pad_maximum_fusion.2
  103.0 0.0 copy-start.6
  103.0 1.0 copy-done.6
  104.0 1.5 collective-permute-start.10
  105.5 0.1 pad_add_fusion.1.index_ref
  105.6 11.3 %norm_rows.1.x_ref = bf16[1024,8192]{1,0:T(8,128)(2,1)S(1)} custom-call(bf16[1024,8192]{1,0:T(8,128)(2,1)} %tokens_ref.1, bf16[1,8192]{1,0:T(2,128)(2,1)S(1)} %reshape.65.gain_ref), custom_call_target="tpu_custom_call" | custom-call | flops 33554432 | bytes 33554432 | tf_op jit(solution)/shard_map/norm_rows/pallas_call | solution.py:71
  117.0 5.8 %copy-done.2 = bf16[1024,8192]{1,0:T(8,128)(2,1)} copy-done((bf16[1024,8192]{1,0:T(8,128)(2,1)}, bf16[1024,8192]{1,0:T(8,128)(2,1)S(1)}, u32[]{:S(2)}) %copy-start.2) | copy-done | bytes 16777240
  122.8 0.7 collective-permute-start.8
  123.4 0.3 collective-permute-start.7
  123.7 1.5 fusion
  125.2 1.6 copy.27
  126.9 7.4 %all-to-all-start.1 = ((bf16[32,2,32,256]{3,2,1,0:T(8,128)(2,1)}), bf16[32,2,32,256]{3,2,1,0:T(8,128)(2,1)}, u32[]{:S(2)}, u32[]{:S(2)}) async-start(bf16[32,2,32,256]{3,2,1,0:T(8,128)(2,1)} %copy.27), calls=%async_computation.1 | async-start | bytes 2097152 | tf_op jit(solution)/shard_map/all_to_all | solution.py:314
  134.3 5.8 %copy-done.3 = bf16[1024,8192]{1,0:T(8,128)(2,1)S(1)} copy-done((bf16[1024,8192]{1,0:T(8,128)(2,1)S(1)}, bf16[1024,8192]{1,0:T(8,128)(2,1)}, u32[]{:S(2)}) %copy-start.3) | copy-done | bytes 16777240
  140.1 4.4 %project.13.refs_4_ = f32[1024,512]{1,0:T(8,128)S(1)} custom-call(s32[12]{0:T(128)S(1)} %pad_add_fusion.4.index_ref, bf16[1024,8192]{1,0:T(8,128)(2,1)S(1)} %copy-done.3, bf16[1024,512]{1,0:T(8,128)(2,1)S(1)} %pad_maximum_fusion.1.refs_0_, bf16[1024,512]{1,0:T(8,128)(2,1)} %collective-permute-done.17.refs_1_, bf16[1024,512]{1,0:T(8,128)(2,1)} %collective-permute-done.20.refs_2_), custom_call_target="tpu_custom_call" | custom-call | flops 3221225472 | bytes 3145728 | tf_op jit(solution)/shard_map/project/pallas_call | solution.py:162
  144.4 2.8 %collective-permute-start.16 = (bf16[1024,512]{1,0:T(8,128)(2,1)}, bf16[1024,512]{1,0:T(8,128)(2,1)S(1)}, u32[]{:S(2)}, u32[]{:S(2)}) collective-permute-start(bf16[1024,512]{1,0:T(8,128)(2,1)} %collective-permute-done.15.refs_3_), channel_id=1, source_target_pairs={{0,48},{16,0},{32,16},{48,32},{1,49},{17,1},{33,17},{49,33},{2,50}... | collective-permute-start | bytes 3145736 | tf_op jit(solution)/shard_map/ppermute | solution.py:29
  147.3 2.7 %collective-permute-start.5 = (bf16[1024,512]{1,0:T(8,128)(2,1)}, bf16[1024,512]{1,0:T(8,128)(2,1)S(1)}, u32[]{:S(2)}, u32[]{:S(2)}) collective-permute-start(bf16[1024,512]{1,0:T(8,128)(2,1)} %collective-permute-done.4.refs_3_), channel_id=1, source_target_pairs={{0,12},{4,0},{8,4},{12,8},{1,13},{5,1},{9,5},{13,9},{2,14},{6,2},{... | collective-permute-start | bytes 3145736 | tf_op jit(solution)/shard_map/ppermute | solution.py:29
  150.0 4.3 %project.8.refs_4_ = f32[1024,512]{1,0:T(8,128)S(1)} custom-call(s32[12]{0:T(128)S(1)} %pad_add_fusion.2.index_ref, bf16[1024,8192]{1,0:T(8,128)(2,1)S(1)} %copy-done.3, bf16[1024,512]{1,0:T(8,128)(2,1)S(1)} %pad_maximum_fusion.refs_0_, bf16[1024,512]{1,0:T(8,128)(2,1)} %collective-permute-done.6.refs_1_, bf16[1024,512]{1,0:T(8,128)(2,1)S(1)} %copy-done.7), custom_call_target="tpu_custom_call" | custom-call | flops 3221225472 | bytes 3145728 | tf_op jit(solution)/shard_map/project/pallas_call | solution.py:162
  154.3 11.9 %project.14.refs_1_ = f32[1024,512]{1,0:T(8,128)S(1)} custom-call(s32[16]{0:T(128)S(1)} %pad_add_fusion.3.index_ref, bf16[1024,8192]{1,0:T(8,128)(2,1)} %copy-done.2, bf16[1024,512]{1,0:T(8,128)(2,1)} %collective-permute-done.18.refs_0_, bf16[1024,512]{1,0:T(8,128)(2,1)S(1)} %collective-permute-done.14.refs_1_, ...), custom_call_target="tpu_custom_call" | custom-call | flops 4294967296 | bytes 4194304 | tf_op jit(solution)/shard_map/project/pallas_call | solution.py:162
  166.3 14.0 %collective-permute-done.7.refs_0_ = bf16[1024,512]{1,0:T(8,128)(2,1)} collective-permute-done((bf16[1024,512]{1,0:T(8,128)(2,1)}, bf16[1024,512]{1,0:T(8,128)(2,1)}, u32[]{:S(2)}, u32[]{:S(2)}) %collective-permute-start.7) | collective-permute-done | bytes 1048608 | tf_op jit(solution)/shard_map/ppermute | solution.py:29
  180.2 11.9 %project.9.refs_1_ = f32[1024,512]{1,0:T(8,128)S(1)} custom-call(s32[16]{0:T(128)S(1)} %pad_add_fusion.1.index_ref, bf16[1024,8192]{1,0:T(8,128)(2,1)} %copy-done.2, bf16[1024,512]{1,0:T(8,128)(2,1)} %collective-permute-done.7.refs_0_, bf16[1024,512]{1,0:T(8,128)(2,1)} %collective-permute-done.3.refs_1_, bf16[1024,512]{1,0:T(8,128)(2,1)} %collective-permute-done.8.refs_2_, ...), custom_call_target="tpu_custom_call" | custom-call | flops 4294967296 | bytes 4194304 | tf_op jit(solution)/shard_map/project/pallas_call | solution.py:162
  192.2 5.8 %copy-done.4 = bf16[1024,8192]{1,0:T(8,128)(2,1)S(1)} copy-done((bf16[1024,8192]{1,0:T(8,128)(2,1)S(1)}, bf16[1024,8192]{1,0:T(8,128)(2,1)}, u32[]{:S(2)}) %copy-start.4) | copy-done | bytes 16777240
  198.0 3.7 %project.15.q_ref = bf16[1024,512]{1,0:T(8,128)(2,1)S(1)} custom-call(s32[4]{0:T(128)S(1)} %get-tuple-element.23.index_ref, bf16[1024,8192]{1,0:T(8,128)(2,1)S(1)} %copy-done.4, bf16[1024,512]{1,0:T(8,128)(2,1)S(1)} %collective-permute-done.16.refs_0_, f32[1024,512]{1,0:T(8,128)S(1)} %project.14.refs_1_, f32[1,512]{1,0:T(1,128)S(1)} %maximum_convert_fusion.1.refs_2_, ...), custom_call_target="tpu_custom_call" | custom-call | flops 1073741824 | bytes 1048576 | tf_op jit(solution)/shard_map/project/pallas_call | solution.py:162
  201.7 3.8 %project.10.q_ref = bf16[1024,512]{1,0:T(8,128)(2,1)S(1)} custom-call(s32[4]{0:T(128)S(1)} %get-tuple-element.32.index_ref, bf16[1024,8192]{1,0:T(8,128)(2,1)S(1)} %copy-done.4, bf16[1024,512]{1,0:T(8,128)(2,1)S(1)} %collective-permute-done.5.refs_0_, f32[1024,512]{1,0:T(8,128)S(1)} %project.9.refs_1_, f32[1,512]{1,0:T(1,128)S(1)} %slice.24.refs_2_, ...), custom_call_target="tpu_custom_call" | custom-call | flops 1073741824 | bytes 1048576 | tf_op jit(solution)/shard_map/project/pallas_call | solution.py:162
  205.4 3.6 %project.11.refs_1_ = f32[1024,256]{1,0:T(8,128)S(1)} custom-call(s32[16]{0:T(128)S(1)} %iota_add_fusion.index_ref, bf16[1024,8192]{1,0:T(8,128)(2,1)S(1)} %copy-done.4, bf16[4096,256]{1,0:T(8,128)(2,1)S(1)} %bitcast.21), custom_call_target="tpu_custom_call" | custom-call | flops 2147483648 | bytes 2097152 | tf_op jit(solution)/shard_map/project/pallas_call | solution.py:162
  209.0 0.0 copy-start.10
  209.0 5.6 %project.12.text_ref = bf16[1024,256]{1,0:T(8,128)(2,1)S(1)} custom-call(s32[16]{0:T(128)S(1)} %iota_add_fusion.1.index_ref, bf16[1024,8192]{1,0:T(8,128)(2,1)S(1)} %copy-done.4, bf16[4096,256]{1,0:T(8,128)(2,1)} %collective-permute-done.10.refs_0_, f32[1024,256]{1,0:T(8,128)S(1)} %project.11.refs_1_, f32[1,256]{1,0:T(1,128)S(1)} %maximum_convert_fusion.2.refs_2_, ...), custom_call_target="tpu_custom_call" | custom-call | flops 2147483648 | bytes 2097152 | tf_op jit(solution)/shard_map/project/pallas_call | solution.py:162
  214.7 0.8 copy-done.8
  215.5 1.0 copy-done.9
  216.5 14.6 %attend.2.refs_0_ = bf16[1024,1024]{1,0:T(8,128)(2,1)} custom-call(s32[16]{0:T(128)S(1)} %add_clamp_fusion.which_ref, s32[16]{0:T(128)S(1)} %copy-done.10, bf16[1024,512]{1,0:T(8,128)(2,1)S(1)} %project.15.q_ref, bf16[1024,256]{1,0:T(8,128)(2,1)S(1)} %copy-done.9, bf16[32,2,32,256]{3,2,1,0:T(8,128)(2,1)} %all-to-all-done.1.visual_ref), custom_call_target="tpu_custom_call" | custom-call | flops 2147483648 | bytes 2097152 | tf_op jit(solution)/shard_map/attend/pallas_call | solution.py:225
  231.1 14.6 %attend.3 = bf16[1024,1024]{1,0:T(8,128)(2,1)} custom-call(s32[16]{0:T(128)S(1)} %add_clamp_fusion.which_ref, s32[16]{0:T(128)S(1)} %copy-done.10, bf16[1024,512]{1,0:T(8,128)(2,1)S(1)} %project.10.q_ref, bf16[1024,256]{1,0:T(8,128)(2,1)S(1)} %copy-done.9, bf16[32,2,32,256]{3,2,1,0:T(8,128)(2,1)} %all-to-all-done.1.visual_ref, ...), custom_call_target="tpu_custom_call", output_to_operand_aliasing={{}: (5, {})} | custom-call | flops 2147483648 | bytes 2097152 | tf_op jit(solution)/shard_map/attend/pallas_call | solution.py:225
  (67 shorter events, 0.2 us)
Async XLA Ops:
  6.5 21.2 %copy-start = (s32[32]{0:T(128)S(1)}, s32[32]{0:T(128)}, u32[]{:S(2)}) copy-start(s32[32]{0:T(128)} %param.20) | copy-start | bytes 388
  6.5 97.4 %all-gather.3.cloned.1.call-start = ((), (), s32[]{:S(2)}) async-start(), calls=%async_computation.2 | async-start | bytes 2228224 | tf_op jit(solution)/shard_map/all_gather | solution.py:283
  7.3 20.4 %copy-start.15 = (bf16[1024]{0:T(1024)(128)(2,1)S(1)}, bf16[1024]{0:T(1024)(128)(2,1)}, u32[]{:S(2)}) copy-start(bf16[1024]{0:T(1024)(128)(2,1)} %param.14) | copy-start | bytes 6148
  8.3 21.0 %collective-permute-start.11 = (bf16[256,512]{1,0:T(8,128)(2,1)S(1)}, bf16[256,512]{1,0:T(8,128)(2,1)S(1)}, u32[]{:S(2)}, u32[]{:S(2)}) collective-permute-start(bf16[256,512]{1,0:T(8,128)(2,1)S(1)} %get-tuple-element.12), channel_id=1, source_target_pairs={{0,4},{4,8},{8,12},{12,0},{1,5},{5,9},{9,13},{13,1},{2,6},{6,10},{... | collective-permute-start | bytes 786440 | tf_op jit(solution)/shard_map/ppermute | solution.py:29
  10.1 19.2 %collective-permute-start.12 = (bf16[256,512]{1,0:T(8,128)(2,1)S(1)}, bf16[256,512]{1,0:T(8,128)(2,1)S(1)}, u32[]{:S(2)}, u32[]{:S(2)}) collective-permute-start(bf16[256,512]{1,0:T(8,128)(2,1)S(1)} %get-tuple-element.12), channel_id=1, source_target_pairs={{0,12},{4,0},{8,4},{12,8},{1,13},{5,1},{9,5},{13,9},{2,14},{6,2},{... | collective-permute-start | bytes 786440 | tf_op jit(solution)/shard_map/ppermute | solution.py:29
  11.6 17.7 %collective-permute-start.13 = (bf16[256,512]{1,0:T(8,128)(2,1)S(1)}, bf16[256,512]{1,0:T(8,128)(2,1)S(1)}, u32[]{:S(2)}, u32[]{:S(2)}) collective-permute-start(bf16[256,512]{1,0:T(8,128)(2,1)S(1)} %get-tuple-element.12), channel_id=1, source_target_pairs={{0,8},{4,12},{8,0},{12,4},{1,9},{5,13},{9,1},{13,5},{2,10},{6,14},... | collective-permute-start | bytes 786440 | tf_op jit(solution)/shard_map/ppermute | solution.py:29
  13.7 15.4 %copy-start.14 = (bf16[1,256]{1,0:T(2,128)(2,1)S(1)}, bf16[1,256]{1,0:T(2,128)(2,1)}, u32[]{:S(2)}) copy-start(bf16[1,256]{1,0:T(2,128)(2,1)} %param.16) | copy-start | bytes 1540
  13.7 15.5 %copy-start.17 = (s32[16]{0:T(128)S(1)}, s32[16]{0:T(128)}, u32[]{:S(2)}) copy-start(s32[16]{0:T(128)} %param.18) | copy-start | bytes 196
  13.7 15.5 %copy-start.16 = (s32[4]{0:T(128)S(1)}, s32[4]{0:T(128)}, u32[]{:S(2)}) copy-start(s32[4]{0:T(128)} %constant.153.clone) | copy-start | bytes 52
  13.7 20.0 %collective-permute-start = (bf16[256,512]{1,0:T(8,128)(2,1)S(1)}, bf16[256,512]{1,0:T(8,128)(2,1)S(1)}, u32[]{:S(2)}, u32[]{:S(2)}) collective-permute-start(bf16[256,512]{1,0:T(8,128)(2,1)S(1)} %get-tuple-element.13), channel_id=1, source_target_pairs={{0,16},{16,32},{32,48},{48,0},{1,17},{17,33},{33,49},{49,1},{2,18}... | collective-permute-start | bytes 786440 | tf_op jit(solution)/shard_map/ppermute | solution.py:29
  15.2 20.4 %collective-permute-start.1 = (bf16[256,512]{1,0:T(8,128)(2,1)S(1)}, bf16[256,512]{1,0:T(8,128)(2,1)S(1)}, u32[]{:S(2)}, u32[]{:S(2)}) collective-permute-start(bf16[256,512]{1,0:T(8,128)(2,1)S(1)} %get-tuple-element.13), channel_id=1, source_target_pairs={{0,48},{16,0},{32,16},{48,32},{1,49},{17,1},{33,17},{49,33},{2,50}... | collective-permute-start | bytes 786440 | tf_op jit(solution)/shard_map/ppermute | solution.py:29
  18.9 104.8 %all-to-all-start = ((bf16[128,8,256]{2,1,0:T(8,128)(2,1)}), bf16[128,8,256]{2,1,0:T(8,128)(2,1)}, u32[]{:S(2)}, u32[]{:S(2)}) async-start(bf16[128,8,256]{2,1,0:T(8,128)(2,1)} %bitcast.8), calls=%async_computation | async-start | bytes 1048576 | tf_op jit(solution)/shard_map/all_to_all | solution.py:306
  29.3 76.3 %copy-start.13 = (bf16[8192]{0:T(1024)(128)(2,1)S(1)}, bf16[8192]{0:T(1024)(128)(2,1)}, u32[]{:S(2)}) copy-start(bf16[8192]{0:T(1024)(128)(2,1)} %param.12) | copy-start | bytes 49156
  29.4 48.0 %collective-permute-start.17 = (bf16[1024,512]{1,0:T(8,128)(2,1)S(1)}, bf16[1024,512]{1,0:T(8,128)(2,1)}, u32[]{:S(2)}, u32[]{:S(2)}) collective-permute-start(bf16[1024,512]{1,0:T(8,128)(2,1)S(1)} %pad_maximum_fusion.1.refs_0_), channel_id=1, source_target_pairs={{0,16},{16,32},{32,48},{48,0},{1,17},{17,33},{33,49},{49,1},{2,18}... | collective-permute-start | bytes 3145736 | tf_op jit(solution)/shard_map/ppermute | solution.py:29
  30.4 50.5 %collective-permute-start.20 = (bf16[1024,512]{1,0:T(8,128)(2,1)S(1)}, bf16[1024,512]{1,0:T(8,128)(2,1)}, u32[]{:S(2)}, u32[]{:S(2)}) collective-permute-start(bf16[1024,512]{1,0:T(8,128)(2,1)S(1)} %pad_maximum_fusion.1.refs_0_), channel_id=1, source_target_pairs={{0,48},{16,0},{32,16},{48,32},{1,49},{17,1},{33,17},{49,33},{2,50}... | collective-permute-start | bytes 3145736 | tf_op jit(solution)/shard_map/ppermute | solution.py:29
  32.7 46.9 %collective-permute-start.14 = (bf16[1024,512]{1,0:T(8,128)(2,1)S(1)}, bf16[1024,512]{1,0:T(8,128)(2,1)S(1)}, u32[]{:S(2)}, u32[]{:S(2)}) collective-permute-start(bf16[1024,512]{1,0:T(8,128)(2,1)S(1)} %pad_maximum_fusion.1.refs_0_), channel_id=1, source_target_pairs={{0,64},{64,0},{1,65},{65,1},{2,66},{66,2},{3,67},{67,3},{4,68},{68... | collective-permute-start | bytes 3145736 | tf_op jit(solution)/shard_map/ppermute | solution.py:29
  33.7 1.9 copy-start.11
  33.7 39.7 %collective-permute-start.2 = (bf16[256,512]{1,0:T(8,128)(2,1)S(1)}, bf16[256,512]{1,0:T(8,128)(2,1)}, u32[]{:S(2)}, u32[]{:S(2)}) collective-permute-start(bf16[256,512]{1,0:T(8,128)(2,1)S(1)} %get-tuple-element.13), channel_id=1, source_target_pairs={{0,32},{16,48},{32,0},{48,16},{1,33},{17,49},{33,1},{49,17},{2,34}... | collective-permute-start | bytes 786440 | tf_op jit(solution)/shard_map/ppermute | solution.py:29
  35.6 0.7 copy-start.12
  74.6 26.4 %collective-permute-start.6 = (bf16[1024,512]{1,0:T(8,128)(2,1)S(1)}, bf16[1024,512]{1,0:T(8,128)(2,1)}, u32[]{:S(2)}, u32[]{:S(2)}) collective-permute-start(bf16[1024,512]{1,0:T(8,128)(2,1)S(1)} %pad_maximum_fusion.refs_0_), channel_id=1, source_target_pairs={{0,4},{4,8},{8,12},{12,0},{1,5},{5,9},{9,13},{13,1},{2,6},{6,10},{... | collective-permute-start | bytes 3145736 | tf_op jit(solution)/shard_map/ppermute | solution.py:29
  75.8 25.8 %collective-permute-start.3 = (bf16[1024,512]{1,0:T(8,128)(2,1)S(1)}, bf16[1024,512]{1,0:T(8,128)(2,1)}, u32[]{:S(2)}, u32[]{:S(2)}) collective-permute-start(bf16[1024,512]{1,0:T(8,128)(2,1)S(1)} %pad_maximum_fusion.refs_0_), channel_id=1, source_target_pairs={{0,64},{64,0},{1,65},{65,1},{2,66},{66,2},{3,67},{67,3},{4,68},{68... | collective-permute-start | bytes 3145736 | tf_op jit(solution)/shard_map/ppermute | solution.py:29
  77.4 25.6 %collective-permute-start.9 = (bf16[1024,512]{1,0:T(8,128)(2,1)S(1)}, bf16[1024,512]{1,0:T(8,128)(2,1)S(1)}, u32[]{:S(2)}, u32[]{:S(2)}) collective-permute-start(bf16[1024,512]{1,0:T(8,128)(2,1)S(1)} %pad_maximum_fusion.refs_0_), channel_id=1, source_target_pairs={{0,12},{4,0},{8,4},{12,8},{1,13},{5,1},{9,5},{13,9},{2,14},{6,2},{... | collective-permute-start | bytes 3145736 | tf_op jit(solution)/shard_map/ppermute | solution.py:29
  79.7 43.1 %collective-permute-start.15 = (bf16[1024,512]{1,0:T(8,128)(2,1)S(1)}, bf16[1024,512]{1,0:T(8,128)(2,1)}, u32[]{:S(2)}, u32[]{:S(2)}) collective-permute-start(bf16[1024,512]{1,0:T(8,128)(2,1)S(1)} %collective-permute-done.14.refs_1_), channel_id=1, source_target_pairs={{0,48},{16,0},{32,16},{48,32},{1,49},{17,1},{33,17},{49,33},{2,50}... | collective-permute-start | bytes 3145736 | tf_op jit(solution)/shard_map/ppermute | solution.py:29
  80.8 42.6 %collective-permute-start.19 = (bf16[1024,512]{1,0:T(8,128)(2,1)S(1)}, bf16[1024,512]{1,0:T(8,128)(2,1)}, u32[]{:S(2)}, u32[]{:S(2)}) collective-permute-start(bf16[1024,512]{1,0:T(8,128)(2,1)S(1)} %collective-permute-done.14.refs_1_), channel_id=1, source_target_pairs={{0,16},{16,32},{32,48},{48,0},{1,17},{17,33},{33,49},{49,1},{2,18}... | collective-permute-start | bytes 3145736 | tf_op jit(solution)/shard_map/ppermute | solution.py:29
  101.0 43.4 %collective-permute-start.18 = (bf16[1024,512]{1,0:T(8,128)(2,1)}, bf16[1024,512]{1,0:T(8,128)(2,1)}, u32[]{:S(2)}, u32[]{:S(2)}) collective-permute-start(bf16[1024,512]{1,0:T(8,128)(2,1)} %collective-permute-done.17.refs_1_), channel_id=1, source_target_pairs={{0,16},{16,32},{32,48},{48,0},{1,17},{17,33},{33,49},{49,1},{2,18}... | collective-permute-start | bytes 3145736 | tf_op jit(solution)/shard_map/ppermute | solution.py:29
  101.6 45.7 %collective-permute-start.4 = (bf16[1024,512]{1,0:T(8,128)(2,1)}, bf16[1024,512]{1,0:T(8,128)(2,1)}, u32[]{:S(2)}, u32[]{:S(2)}) collective-permute-start(bf16[1024,512]{1,0:T(8,128)(2,1)} %collective-permute-done.3.refs_1_), channel_id=1, source_target_pairs={{0,12},{4,0},{8,4},{12,8},{1,13},{5,1},{9,5},{13,9},{2,14},{6,2},{... | collective-permute-start | bytes 3145736 | tf_op jit(solution)/shard_map/ppermute | solution.py:29
  103.0 1.0 copy-start.6
  104.0 105.1 %collective-permute-start.10 = (bf16[4096,256]{1,0:T(8,128)(2,1)}, bf16[4096,256]{1,0:T(8,128)(2,1)}, u32[]{:S(2)}, u32[]{:S(2)}) collective-permute-start(bf16[4096,256]{1,0:T(8,128)(2,1)} %bitcast.20), channel_id=1, source_target_pairs={{0,64},{64,0},{1,65},{65,1},{2,66},{66,2},{3,67},{67,3},{4,68},{68... | collective-permute-start | bytes 6291464 | tf_op jit(solution)/shard_map/ppermute | solution.py:29
  117.0 5.8 %copy-start.2 = (bf16[1024,8192]{1,0:T(8,128)(2,1)}, bf16[1024,8192]{1,0:T(8,128)(2,1)S(1)}, u32[]{:S(2)}) copy-start(bf16[1024,8192]{1,0:T(8,128)(2,1)S(1)} %norm_rows.1.x_ref) | copy-start | bytes 50331652
  122.8 43.5 %collective-permute-start.8 = (bf16[1024,512]{1,0:T(8,128)(2,1)}, bf16[1024,512]{1,0:T(8,128)(2,1)}, u32[]{:S(2)}, u32[]{:S(2)}) collective-permute-start(bf16[1024,512]{1,0:T(8,128)(2,1)} %collective-permute-done.3.refs_1_), channel_id=1, source_target_pairs={{0,4},{4,8},{8,12},{12,0},{1,5},{5,9},{9,13},{13,1},{2,6},{6,10},{... | collective-permute-start | bytes 3145736 | tf_op jit(solution)/shard_map/ppermute | solution.py:29
  123.4 56.8 %collective-permute-start.7 = (bf16[1024,512]{1,0:T(8,128)(2,1)}, bf16[1024,512]{1,0:T(8,128)(2,1)}, u32[]{:S(2)}, u32[]{:S(2)}) collective-permute-start(bf16[1024,512]{1,0:T(8,128)(2,1)} %collective-permute-done.6.refs_1_), channel_id=1, source_target_pairs={{0,4},{4,8},{8,12},{12,0},{1,5},{5,9},{9,13},{13,1},{2,6},{6,10},{... | collective-permute-start | bytes 3145736 | tf_op jit(solution)/shard_map/ppermute | solution.py:29
  126.9 88.6 %all-to-all-start.1 = ((bf16[32,2,32,256]{3,2,1,0:T(8,128)(2,1)}), bf16[32,2,32,256]{3,2,1,0:T(8,128)(2,1)}, u32[]{:S(2)}, u32[]{:S(2)}) async-start(bf16[32,2,32,256]{3,2,1,0:T(8,128)(2,1)} %copy.27), calls=%async_computation.1 | async-start | bytes 2097152 | tf_op jit(solution)/shard_map/all_to_all | solution.py:314
  134.3 5.8 %copy-start.3 = (bf16[1024,8192]{1,0:T(8,128)(2,1)S(1)}, bf16[1024,8192]{1,0:T(8,128)(2,1)}, u32[]{:S(2)}) copy-start(bf16[1024,8192]{1,0:T(8,128)(2,1)} %copy-done.2) | copy-start | bytes 50331652
  140.1 9.9 %copy-start.7 = (bf16[1024,512]{1,0:T(8,128)(2,1)S(1)}, bf16[1024,512]{1,0:T(8,128)(2,1)}, u32[]{:S(2)}) copy-start(bf16[1024,512]{1,0:T(8,128)(2,1)} %copy-done.6) | copy-start | bytes 3145732
  144.4 47.7 %collective-permute-start.16 = (bf16[1024,512]{1,0:T(8,128)(2,1)}, bf16[1024,512]{1,0:T(8,128)(2,1)S(1)}, u32[]{:S(2)}, u32[]{:S(2)}) collective-permute-start(bf16[1024,512]{1,0:T(8,128)(2,1)} %collective-permute-done.15.refs_3_), channel_id=1, source_target_pairs={{0,48},{16,0},{32,16},{48,32},{1,49},{17,1},{33,17},{49,33},{2,50}... | collective-permute-start | bytes 3145736 | tf_op jit(solution)/shard_map/ppermute | solution.py:29
  147.3 54.4 %collective-permute-start.5 = (bf16[1024,512]{1,0:T(8,128)(2,1)}, bf16[1024,512]{1,0:T(8,128)(2,1)S(1)}, u32[]{:S(2)}, u32[]{:S(2)}) collective-permute-start(bf16[1024,512]{1,0:T(8,128)(2,1)} %collective-permute-done.4.refs_3_), channel_id=1, source_target_pairs={{0,12},{4,0},{8,4},{12,8},{1,13},{5,1},{9,5},{13,9},{2,14},{6,2},{... | collective-permute-start | bytes 3145736 | tf_op jit(solution)/shard_map/ppermute | solution.py:29
  192.2 5.8 %copy-start.4 = (bf16[1024,8192]{1,0:T(8,128)(2,1)S(1)}, bf16[1024,8192]{1,0:T(8,128)(2,1)}, u32[]{:S(2)}) copy-start(bf16[1024,8192]{1,0:T(8,128)(2,1)} %copy-done.2) | copy-start | bytes 50331652
  201.7 3.8 %copy-start.5 = (bf16[4096,1,256]{2,0,1:T(8,128)(2,1)S(1)}, bf16[4096,1,256]{2,0,1:T(8,128)(2,1)}, u32[]{:S(2)}) copy-start(bf16[4096,1,256]{2,0,1:T(8,128)(2,1)} %all-gather.3.cloned.1.call-done) | copy-start | bytes 6291460
  209.0 6.5 %copy-start.10 = (s32[16]{0:T(128)S(1)}, s32[16]{0:T(128)}, u32[]{:S(2)}) copy-start(s32[16]{0:T(128)} %len_ref.3) | copy-start | bytes 196
  214.7 0.8 copy-start.8
  215.5 1.0 copy-start.9
  216.5 29.1 %copy-start.1 = (s32[32]{0:T(128)S(1)}, s32[32]{0:T(128)}, u32[]{:S(2)}) copy-start(s32[32]{0:T(128)} %param.20) | copy-start | bytes 388
Sparse Core Ops, SparseCore 0:
  9.5 56.3 all-gather.2

commit v3 on v2

--- a/solution.py
+++ b/solution.py
@@ -29,55 +29,38 @@
     return lax.ppermute(value, axis, [(i, (i + by) % size) for i in range(size)])
 
 
+def after(value, *others):
+    return lax.optimization_barrier((value, others))[0]
+
+
 def whole():
     return pl.BlockSpec(memory_space=pltpu.VMEM)
 
 
-def norm_body(tokens_ref, gain_ref, out_ref, buf, sems):
-    rows = tokens_ref.shape[0]
-    depth, tile = buf.shape[:2]
-    count = rows // tile
-
-    def copy(i, slot):
-        at = pl.multiple_of(i * tile, tile)
-        return pltpu.make_async_copy(tokens_ref.at[pl.ds(at, tile)], buf.at[slot], sems.at[slot])
-
-    for i in range(depth - 1):
-        copy(i, i).start()
+def norm_body(tokens_ref, gain_ref, out_ref):
     gain = gain_ref[...].astype(jnp.float32)
-
-    def one(i, carry):
-        slot = lax.rem(i, depth)
-
-        @pl.when(i + depth - 1 < count)
-        def _():
-            copy(i + depth - 1, lax.rem(i + depth - 1, depth)).start()
-
-        copy(i, slot).wait()
-        for part in range(tile // 16):
-            wide = buf[slot, part * 16 : (part + 1) * 16, :].astype(jnp.float32)
-            mean_square = jnp.mean(wide * wide, -1, keepdims=True)
-            out_ref[pl.ds(pl.multiple_of(i * tile + part * 16, 16), 16), :] = (
-                wide * lax.rsqrt(mean_square + 1e-06) * gain
-            ).astype(jnp.bfloat16)
-        return carry
-
-    lax.fori_loop(0, count, one, 0)
+    for first in range(0, tokens_ref.shape[0], 16):
+        rows = slice(first, first + 16)
+        wide = tokens_ref[rows, :].astype(jnp.float32)
+        mean_square = jnp.mean(wide * wide, -1, keepdims=True)
+        normed = (wide * lax.rsqrt(mean_square + 1e-06) * gain).astype(jnp.bfloat16)
+        for j in range(out_ref.shape[0]):
+            out_ref[j, rows, :] = normed[:, j * PIECE : (j + 1) * PIECE]
 
 
 def norm_rows(tokens, gain):
     rows, width = tokens.shape
-    depth, tile = 4, 64
+    tile = 64
     return pl.pallas_call(
         norm_body,
-        in_specs=[pl.BlockSpec(memory_space=pl.ANY), whole()],
-        out_specs=whole(),
-        out_shape=jax.ShapeDtypeStruct((rows, width), jnp.bfloat16),
-        scratch_shapes=[
-            pltpu.VMEM((depth, tile, width), jnp.bfloat16),
-            pltpu.SemaphoreType.DMA((depth,)),
+        grid=(rows // tile,),
+        in_specs=[
+            pl.BlockSpec((tile, width), lambda i: (i, 0)),
+            pl.BlockSpec((1, width), lambda i: (0, 0)),
         ],
-        compiler_params=pltpu.CompilerParams(vmem_limit_bytes=24 * MIB),
+        out_specs=pl.BlockSpec((width // PIECE, tile, PIECE), lambda i: (0, i, 0)),
+        out_shape=jax.ShapeDtypeStruct((width // PIECE, rows, PIECE), jnp.bfloat16),
+        compiler_params=pltpu.CompilerParams(vmem_limit_bytes=60 * MIB),
         cost_estimate=pl.CostEstimate(
             flops=4 * rows * width, bytes_accessed=4 * rows * width, transcendentals=rows
         ),
@@ -91,9 +74,10 @@
     acc_in = refs.pop(0) if has_acc else None
     if units:
         bias_ref, cos_ref, sin_ref = refs.pop(0), refs.pop(0), refs.pop(0)
-    out_ref, w_buf, sems = refs.pop(0), refs.pop(0), refs.pop(0)
-    acc = refs.pop(0) if units else out_ref
+    out_ref, w_buf, x_buf, acc, w_sems, x_sems, acc_sem = refs
     steps = sum(rows_of) // STEP
+    each = STEP // PIECE
+    slots = x_buf.shape[0]
 
     copies = [[] for _ in range(steps)]
     at = 0
@@ -106,31 +90,47 @@
                 pltpu.make_async_copy(
                     ref.at[pl.ds(done, size)],
                     w_buf.at[pl.ds(at, size)],
-                    sems.at[s, len(copies[s])],
+                    w_sems.at[s, len(copies[s])],
                 )
             )
             done += size
             at += size
-    for group in copies:
-        for copy in group:
+
+    def x_copies(s):
+        return [
+            pltpu.make_async_copy(
+                x_ref.at[index_ref[each * s + j]], x_buf.at[s % slots, j], x_sems.at[s % slots, j]
+            )
+            for j in range(each)
+        ]
+
+    for s in range(steps):
+        for copy in copies[s]:
             copy.start()
+        if s < slots:
+            for copy in x_copies(s):
+                copy.start()
+        if s == 0 and has_acc:
+            load = pltpu.make_async_copy(acc_in, acc, acc_sem)
+            load.start()
 
     tile = 256
     for s in range(steps):
-        for copy in copies[s]:
+        for copy in copies[s] + x_copies(s):
             copy.wait()
+        if s == 0 and has_acc:
+            load.wait()
         w = w_buf.at[pl.ds(s * STEP, STEP)]
-        cols = [
-            pl.ds(pl.multiple_of(index_ref[4 * s + j] * PIECE, PIECE), PIECE) for j in range(4)
-        ]
-        for m in range(0, x_ref.shape[0], tile):
-            x = jnp.concatenate([x_ref[m : m + tile, c] for c in cols], axis=1)
+        for m in range(0, acc.shape[0], tile):
+            rows = slice(m, m + tile)
+            x = jnp.concatenate([x_buf[s % slots, j, rows, :] for j in range(each)], axis=1)
             part = jnp.dot(x, w[...], preferred_element_type=jnp.float32)
-            if s > 0:
-                part += acc[m : m + tile, :]
-            elif has_acc:
-                part += acc_in[m : m + tile, :]
-            acc[m : m + tile, :] = part
+            if s > 0 or has_acc:
+                part += acc[rows, :]
+            acc[rows, :] = part
+        if s + slots < steps:
+            for copy in x_copies(s + slots):
+                copy.start()
 
     if units:
 
@@ -145,31 +145,40 @@
             return carry
 
         lax.fori_loop(0, out_ref.shape[0] // 64, rope, 0)
+    else:
+        store = pltpu.make_async_copy(acc, out_ref, acc_sem)
+        store.start()
+        store.wait()
 
 
 def project(normed, index, weights, acc=None, units=None, tail=()):
-    rows = normed.shape[0]
+    rows = normed.shape[1]
     width = weights[0].shape[1]
     rows_of = [w.shape[0] for w in weights]
     total = sum(rows_of)
-    scratch = [
-        pltpu.VMEM((total, width), jnp.bfloat16),
-        pltpu.SemaphoreType.DMA((total // STEP, 4)),
-    ]
-    if units:
-        scratch.append(pltpu.VMEM((rows, width), jnp.float32))
+    slots = min(3, total // STEP)
     accs = [] if acc is None else [acc]
+    anywhere = pl.BlockSpec(memory_space=pl.ANY)
     return pl.pallas_call(
         functools.partial(project_body, rows_of, acc is not None, units),
-        in_specs=[pl.BlockSpec(memory_space=pltpu.SMEM), whole()]
-        + [pl.BlockSpec(memory_space=pl.ANY)] * len(weights)
-        + [whole()] * (len(accs) + len(tail)),
-        out_specs=whole(),
+        in_specs=[pl.BlockSpec(memory_space=pltpu.SMEM)]
+        + [anywhere] * (1 + len(weights) + len(accs))
+        + [whole()] * len(tail),
+        out_specs=whole() if units else anywhere,
         out_shape=jax.ShapeDtypeStruct((rows, width), jnp.bfloat16 if units else jnp.float32),
-        scratch_shapes=scratch,
-        compiler_params=pltpu.CompilerParams(vmem_limit_bytes=30 * MIB),
+        scratch_shapes=[
+            pltpu.VMEM((total, width), jnp.bfloat16),
+            pltpu.VMEM((slots, STEP // PIECE, rows, PIECE), jnp.bfloat16),
+            pltpu.VMEM((rows, width), jnp.float32),
+            pltpu.SemaphoreType.DMA((total // STEP, 4)),
+            pltpu.SemaphoreType.DMA((slots, STEP // PIECE)),
+            pltpu.SemaphoreType.DMA(()),
+        ],
+        compiler_params=pltpu.CompilerParams(vmem_limit_bytes=60 * MIB),
         cost_estimate=pl.CostEstimate(
-            flops=2 * rows * total * width, bytes_accessed=2 * total * width, transcendentals=0
+            flops=2 * rows * total * width,
+            bytes_accessed=2 * total * (width + rows) + 8 * rows * width,
+            transcendentals=0,
         ),
         name="project",
     )(index, normed, *weights, *accs, *tail)
@@ -239,7 +248,7 @@
         ),
         out_shape=jax.ShapeDtypeStruct((rows, out_width), jnp.bfloat16),
         input_output_aliases={5: 0} if befores else {},
-        compiler_params=pltpu.CompilerParams(vmem_limit_bytes=24 * MIB),
+        compiler_params=pltpu.CompilerParams(vmem_limit_bytes=60 * MIB),
         cost_estimate=pl.CostEstimate(
             flops=4 * rows * width * relays * chunk,
             bytes_accessed=4 * rows * width,
@@ -281,21 +290,11 @@
     w_d, w_b, w_c = (pick(weight, s) for s in (SET_D, SET_B, SET_C))
 
     d_own = lax.all_gather(w_d, PLANE, axis=0, tiled=True)
+    cz = shift(w_c, "zl", 1)
     line_b = line_gather(w_b, "y")
     line_c = line_gather(w_c, "x")
+    cross_c = line_gather(cz, "x")
     cross_b = shift(line_b, "zl", 1)
-    cross_c = shift(line_c, "zl", 1)
-    d_cross = shift(d_own, "zl", 1)
-
-    def big(line, cross, axis):
-        own_before, own_after = shift(line, axis, 1), shift(line, axis, -1)
-        own_far = shift(own_before, axis, 1)
-        cross_before, cross_after = shift(cross, axis, 1), shift(cross, axis, -1)
-        cross_far = shift(cross_after, axis, -1)
-        return [line, own_before, own_after], [own_far, cross, cross_before, cross_after], cross_far
-
-    parts_b = big(line_b, cross_b, "x")
-    parts_c = big(line_c, cross_c, "y")
 
     tok_local = visual_keyval.shape[1]
     kv_heads = visual_keyval.shape[2]
@@ -304,6 +303,20 @@
     spread = visual_keyval.reshape(images, chunk, kv_heads, 2 * head_dim).transpose(0, 2, 1, 3)
     spread = spread.reshape(images * kv_heads, chunk, 2 * head_dim)
     held = lax.all_to_all(spread, DP + MP, split_axis=0, concat_axis=0, tiled=True)
+
+    b_before, b_after = shift(line_b, "x", 1), shift(line_b, "x", -1)
+    c_before, c_after = shift(line_c, "y", 1), shift(line_c, "y", -1)
+    normed = norm_rows(tokens, after(norm_gain, line_b, line_c))
+
+    cross_b, cross_c, b_before, b_after, c_before, c_after, held, d_own = (
+        after(v, normed)
+        for v in (cross_b, cross_c, b_before, b_after, c_before, c_after, held, d_own)
+    )
+    d_cross = shift(d_own, "zl", 1)
+    cc_before, cc_after = shift(cross_c, "y", 1), shift(cross_c, "y", -1)
+    cb_before, cb_after = shift(cross_b, "x", 1), shift(cross_b, "x", -1)
+    b_far, c_far = shift(b_before, "x", 1), shift(c_before, "y", 1)
+
     held = held.reshape(images, kv_heads * chunk, 2 * head_dim)
     target = jnp.arange(images, dtype=jnp.int32)
     wanted = jnp.stack([image_owner[jnp.maximum(target - 1, 0)], image_owner[target]], axis=1)
@@ -326,38 +339,44 @@
     def tail(units):
         return pick(bias, units), cos, sin
 
-    normed = norm_rows(tokens, norm_gain)
     turn = jnp.array([0, -1, 1, 2], jnp.int32)
     other = 1 - zl
-
-    def line_of_b(plane, by):
-        return plane * 16 + (x + by) % 4 * 4 + (y + turn) % 4
-
-    def line_of_c(plane, by):
-        return plane * 16 + (x + turn) % 4 * 4 + (y + by) % 4
-
-    def ring_project(units, line_of, parts):
-        early, later, final = parts
-        acc = project(
-            normed, jnp.concatenate([line_of(zl, 0), line_of(zl, -1), line_of(zl, 1)]), early
-        )
-        acc = project(
-            normed,
-            jnp.concatenate(
-                [line_of(zl, 2), line_of(other, 0), line_of(other, -1), line_of(other, 1)]
-            ),
-            later,
-            acc,
-        )
-        return project(normed, line_of(other, 2), [final], acc, units, tail(units))
-
     span = jnp.arange(16, dtype=jnp.int32)
+
+    def lines_b(plane, *bys):
+        return jnp.concatenate([plane * 16 + (x + by) % 4 * 4 + (y + turn) % 4 for by in bys])
+
+    def lines_c(plane, *bys):
+        return jnp.concatenate([plane * 16 + (x + turn) % 4 * 4 + (y + by) % 4 for by in bys])
+
+    acc_b = project(normed, lines_b(zl, 0, -1, 1), [line_b, b_before, b_after])
+    acc_c = project(normed, lines_c(zl, 0, -1, 1), [line_c, c_before, c_after])
     acc_d = project(normed, zl * 16 + span, [d_own])
+    cb_before, cb_after, cc_before, cc_after, b_far, c_far = (
+        after(v, acc_b, acc_c, acc_d)
+        for v in (cb_before, cb_after, cc_before, cc_after, b_far, c_far)
+    )
+    cb_far, cc_far = shift(cb_after, "x", -1), shift(cc_after, "y", -1)
+    acc_b = project(
+        normed,
+        jnp.concatenate([lines_b(zl, 2), lines_b(other, 0, -1, 1)]),
+        [b_far, cross_b, cb_before, cb_after],
+        acc_b,
+    )
+    acc_c = project(
+        normed,
+        jnp.concatenate([lines_c(zl, 2), lines_c(other, 0, -1, 1)]),
+        [c_far, cross_c, cc_before, cc_after],
+        acc_c,
+    )
+    cb_far, cc_far, d_cross, visual = (
+        after(v, acc_b, acc_c) for v in (cb_far, cc_far, d_cross, visual)
+    )
     text = project(normed, other * 16 + span, [d_cross], acc_d, SET_D, tail(SET_D))
-    q_b = ring_project(SET_B, line_of_b, parts_b)
+    q_b = project(normed, lines_b(other, 2), [cb_far], acc_b, SET_B, tail(SET_B))
     width = query_weight.shape[1]
     out = attend(which, caption_length, q_b, text, visual, 0, width)
-    q_c = ring_project(SET_C, line_of_c, parts_c)
+    q_c = project(normed, lines_c(other, 2), [cc_far], acc_c, SET_C, tail(SET_C))
     return attend(which, caption_length, q_c, text, visual, 1, width, out)
 
 

time: 254 us -> 253 us (level)
  Pallas kernels: 89.7 us -> 123 us
  waiting for transfers between devices: 70.9 us -> 42.6 us
  local copies, waits for them, and re-layouts: 26.9 us -> 9.57 us
  other arithmetic: 1.94 us -> 8.48 us
  starting transfers between devices: 47.7 us -> 50.7 us
    ppermute x21 -> x24, waiting for transfers between devices: 70.2 us -> 41.8 us  [shift(): lax.ppermute(value, axis, [(i, (i + by) % size) for i in range(size)])]
    pallas_call x8, Pallas kernels: 49.2 us -> 70.5 us  [project(): pl.pallas_call(functools.partial(project_body, rows_of, acc is not None,...]
    unnamed x37 -> x25, local copies, waits for them, and re-layouts: 21.9 us -> 3.45 us
    pallas_call x1, Pallas kernels: 11.3 us -> 19.8 us  [norm_rows(): pl.pallas_call(norm_body, grid=(rows // tile,), in_specs=[pl.BlockSpec((t...]
    ppermute x21 -> x24, starting transfers between devices: 31.5 us -> 36 us  [shift(): lax.ppermute(value, axis, [(i, (i + by) % size) for i in range(size)])]
    pallas_call x2, Pallas kernels: 29.1 us -> 32.5 us  [attend(): pl.pallas_call(functools.partial(attend_body, length, before is not None)...]
  transfers between devices with their start and end apart: 24 -> 27, of which waited for: 3 -> 5; matrix products, arithmetic and copies ran while one was open for 4% -> 7% of each run, Pallas kernels for 24% -> 32%
where the time goes in v3:
time: 253 us; the launch traced here: 249 us
  Pallas kernels  123 us (49%)
  starting transfers between devices  50.7 us (20%)
  waiting for transfers between devices  42.6 us (17%)
  between operations  13.9 us (5%)
  local copies, waits for them, and re-layouts  9.57 us (4%)
  other arithmetic  8.48 us (3%)
    pallas_call x8, Pallas kernels, project(): pl.pallas_call(functools.partial(project_body, rows_of, acc is not None,...  70.5 us
    ppermute x24, waiting for transfers between devices, shift(): lax.ppermute(value, axis, [(i, (i + by) % size) for i in range(size)])  41.8 us
    ppermute x24, starting transfers between devices, shift(): lax.ppermute(value, axis, [(i, (i + by) % size) for i in range(size)])  36 us
    pallas_call x2, Pallas kernels, attend(): pl.pallas_call(functools.partial(attend_body, length, before is not None)...  32.5 us
    pallas_call x1, Pallas kernels, norm_rows(): pl.pallas_call(norm_body, grid=(rows // tile,), in_specs=[pl.BlockSpec((t...  19.8 us
    all_to_all x1, starting transfers between devices, on_device(): lax.all_to_all(spread, DP + MP, split_axis=0, concat_axis=0, tiled=True)  9.07 us
    all_to_all x1, starting transfers between devices, on_device(): visual = lax.all_to_all(sent, DP, split_axis=0, concat_axis=0, tiled=True)  5.55 us
  transfers between devices with their start and end apart: 27, of which 5 were waited for; matrix products, arithmetic and copies ran while one was open for 7% of the time, Pallas kernels for 32%

profile of v3, /device:TPU:0, one launch (start us, length us, event | category | flops | bytes accessed | tf_op | source)
XLA Modules:
  0.0 249.4 jit_solution(1923241395142868888)
XLA Ops:
  6.5 0.7 all-gather.3.cloned.1.call-update
  7.3 1.1 fusion.11
  8.3 1.6 collective-permute-start.3
  10.0 1.7 collective-permute-start.4
  11.7 1.9 collective-permute-start.5
  13.5 1.6 collective-permute-start
  15.1 1.7 collective-permute-start.1
  16.8 1.1 copy.28
  17.9 0.9 copy.17
  18.8 9.1 %all-to-all-start = ((bf16[128,8,256]{2,1,0:T(8,128)(2,1)}), bf16[128,8,256]{2,1,0:T(8,128)(2,1)}, u32[]{:S(2)}, u32[]{:S(2)}) async-start(bf16[128,8,256]{2,1,0:T(8,128)(2,1)} %bitcast.8), calls=%async_computation | async-start | bytes 1048576 | tf_op jit(solution)/shard_map/all_to_all | solution.py:305
  27.9 0.5 broadcast_add_fusion
  28.4 0.6 broadcast_add_fusion.7
  29.0 2.4 collective-permute-start.2
  31.4 0.6 iota_add_fusion.1.index_ref
  32.0 1.8 collective-permute-start.6
  33.9 0.7 collective-permute-start.13
  34.6 8.6 %collective-permute-done.2 = bf16[256,512]{1,0:T(8,128)(2,1)S(1)} collective-permute-done((bf16[256,512]{1,0:T(8,128)(2,1)S(1)}, bf16[256,512]{1,0:T(8,128)(2,1)S(1)}, u32[]{:S(2)}, u32[]{:S(2)}) %collective-permute-start.2) | collective-permute-done | bytes 262176 | tf_op jit(solution)/shard_map/ppermute | solution.py:29
  43.3 1.4 collective-permute-start.17
  44.8 1.1 collective-permute-start.7
  45.8 2.2 collective-permute-start.8
  48.1 0.5 iota_add_fusion.index_ref
  48.6 1.4 collective-permute-start.9
  50.0 0.6 pad_add_fusion.2.index_ref
  50.6 6.9 %collective-permute-done.7 = bf16[256,512]{1,0:T(8,128)(2,1)S(1)} collective-permute-done((bf16[256,512]{1,0:T(8,128)(2,1)S(1)}, bf16[256,512]{1,0:T(8,128)(2,1)S(1)}, u32[]{:S(2)}, u32[]{:S(2)}) %collective-permute-start.7) | collective-permute-done | bytes 262176 | tf_op jit(solution)/shard_map/ppermute | solution.py:29
  57.5 4.6 %collective-permute-done.8 = bf16[256,512]{1,0:T(8,128)(2,1)S(1)} collective-permute-done((bf16[256,512]{1,0:T(8,128)(2,1)S(1)}, bf16[256,512]{1,0:T(8,128)(2,1)S(1)}, u32[]{:S(2)}, u32[]{:S(2)}) %collective-permute-start.8) | collective-permute-done | bytes 262176 | tf_op jit(solution)/shard_map/ppermute | solution.py:29
  62.2 0.6 pad_add_fusion.1.index_ref
  62.8 0.6 reshape.65.gain_ref
  63.4 19.8 %norm_rows.1.x_ref = bf16[32,1024,256]{2,1,0:T(8,128)(2,1)} custom-call(bf16[1024,8192]{1,0:T(8,128)(2,1)} %tokens_ref.1, bf16[1,8192]{1,0:T(2,128)(2,1)} %reshape.65.gain_ref), custom_call_target="tpu_custom_call" | custom-call | flops 33554432 | bytes 33554432 | tf_op jit(solution)/shard_map/norm_rows/pallas_call | solution.py:54
  83.2 4.5 %collective-permute-start.12 = (bf16[1024,512]{1,0:T(8,128)(2,1)S(1)}, bf16[1024,512]{1,0:T(8,128)(2,1)}, u32[]{:S(2)}, u32[]{:S(2)}) collective-permute-start(bf16[1024,512]{1,0:T(8,128)(2,1)S(1)} %pad_maximum_fusion.refs_0_), channel_id=1, source_target_pairs={{0,48},{16,0},{32,16},{48,32},{1,49},{17,1},{33,17},{49,33},{2,50}... | collective-permute-start | bytes 3145736 | tf_op jit(solution)/shard_map/ppermute | solution.py:29
  87.8 1.0 pad_maximum_fusion.2.refs_1_
  88.8 0.1 collective-permute-start.10
  88.9 2.1 collective-permute-start.19
  91.0 0.7 pad_add_fusion.4.index_ref
  91.6 0.7 gather_fusion
  92.3 0.7 gather_fusion.1
  93.1 0.5 maximum_convert_fusion.2.refs_2_
  93.6 0.2 fusion.6
  93.8 2.0 collective-permute-start.21
  95.8 0.1 collective-permute-start.20
  95.9 0.6 pad_add_fusion.3.index_ref
  96.5 0.6 slice.24.refs_2_
  97.1 0.6 maximum_convert_fusion.1.refs_2_
  97.7 0.7 pad_maximum_fusion.3
  98.4 12.9 %collective-permute-done.12.refs_2_ = bf16[1024,512]{1,0:T(8,128)(2,1)} collective-permute-done((bf16[1024,512]{1,0:T(8,128)(2,1)S(1)}, bf16[1024,512]{1,0:T(8,128)(2,1)}, u32[]{:S(2)}, u32[]{:S(2)}) %collective-permute-start.12) | collective-permute-done | bytes 1048608 | tf_op jit(solution)/shard_map/ppermute | solution.py:29
  111.4 2.0 collective-permute-start.18
  113.4 2.0 collective-permute-start.16
  115.4 8.8 %collective-permute-done.19.refs_3_ = bf16[1024,512]{1,0:T(8,128)(2,1)} collective-permute-done((bf16[1024,512]{1,0:T(8,128)(2,1)}, bf16[1024,512]{1,0:T(8,128)(2,1)}, u32[]{:S(2)}, u32[]{:S(2)}) %collective-permute-start.19) | collective-permute-done | bytes 1048608 | tf_op jit(solution)/shard_map/ppermute | solution.py:29
  124.1 8.4 %project.9.refs_4_ = f32[1024,512]{1,0:T(8,128)} custom-call(s32[12]{0:T(128)} %pad_add_fusion.2.index_ref, bf16[32,1024,256]{2,1,0:T(8,128)(2,1)} %norm_rows.1.x_ref, bf16[1024,512]{1,0:T(8,128)(2,1)} %copy-done.2, bf16[1024,512]{1,0:T(8,128)(2,1)} %collective-permute-done.13.refs_1_, bf16[1024,512]{1,0:T(8,128)(2,1)} %collective-permute-done.14.refs_2_), custom_call_target="tpu_custom_call" | custom-call | flops 3221225472 | bytes 13631488 | tf_op jit(solution)/shard_map/project/pallas_call | solution.py:162
  132.5 8.4 %project.8.refs_4_ = f32[1024,512]{1,0:T(8,128)} custom-call(s32[12]{0:T(128)} %pad_add_fusion.1.index_ref, bf16[32,1024,256]{2,1,0:T(8,128)(2,1)} %norm_rows.1.x_ref, bf16[1024,512]{1,0:T(8,128)(2,1)} %copy-done.3, bf16[1024,512]{1,0:T(8,128)(2,1)} %collective-permute-done.11.refs_1_, bf16[1024,512]{1,0:T(8,128)(2,1)} %collective-permute-done.12.refs_2_), custom_call_target="tpu_custom_call" | custom-call | flops 3221225472 | bytes 13631488 | tf_op jit(solution)/shard_map/project/pallas_call | solution.py:162
  141.0 7.1 %project.10.refs_1_ = f32[1024,256]{1,0:T(8,128)} custom-call(s32[16]{0:T(128)} %iota_add_fusion.1.index_ref, bf16[32,1024,256]{2,1,0:T(8,128)(2,1)} %norm_rows.1.x_ref, bf16[4096,256]{1,0:T(8,128)(2,1)} %bitcast.22), custom_call_target="tpu_custom_call" | custom-call | flops 2147483648 | bytes 12582912 | tf_op jit(solution)/shard_map/project/pallas_call | solution.py:162
  148.1 3.8 %collective-permute-start.23 = (bf16[1024,512]{1,0:T(8,128)(2,1)}, bf16[1024,512]{1,0:T(8,128)(2,1)S(1)}, u32[]{:S(2)}, u32[]{:S(2)}) collective-permute-start(bf16[1024,512]{1,0:T(8,128)(2,1)} %collective-permute-done.19.refs_3_), channel_id=1, source_target_pairs={{0,48},{16,0},{32,16},{48,32},{1,49},{17,1},{33,17},{49,33},{2,50}... | collective-permute-start | bytes 3145736 | tf_op jit(solution)/shard_map/ppermute | solution.py:29
  151.8 1.5 fusion
  153.4 1.5 copy.27
  154.9 5.5 %all-to-all-start.1 = ((bf16[32,2,32,256]{3,2,1,0:T(8,128)(2,1)}), bf16[32,2,32,256]{3,2,1,0:T(8,128)(2,1)}, u32[]{:S(2)}, u32[]{:S(2)}) async-start(bf16[32,2,32,256]{3,2,1,0:T(8,128)(2,1)} %copy.27), calls=%async_computation.1 | async-start | bytes 2097152 | tf_op jit(solution)/shard_map/all_to_all | solution.py:327
  160.5 0.6 add_clamp_fusion.which_ref
  161.1 11.3 %project.12.refs_1_ = f32[1024,512]{1,0:T(8,128)} custom-call(s32[16]{0:T(128)} %pad_add_fusion.4.index_ref, bf16[32,1024,256]{2,1,0:T(8,128)(2,1)} %norm_rows.1.x_ref, bf16[1024,512]{1,0:T(8,128)(2,1)} %collective-permute-done.20.refs_0_, bf16[1024,512]{1,0:T(8,128)(2,1)} %copy-done.4, bf16[1024,512]{1,0:T(8,128)(2,1)} %collective-permute-done.21.refs_2_, ...), custom_call_target="tpu_custom_call" | custom-call | flops 4294967296 | bytes 16777216 | tf_op jit(solution)/shard_map/project/pallas_call | solution.py:162
  172.4 11.3 %project.11.refs_1_ = f32[1024,512]{1,0:T(8,128)} custom-call(s32[16]{0:T(128)} %pad_add_fusion.3.index_ref, bf16[32,1024,256]{2,1,0:T(8,128)(2,1)} %norm_rows.1.x_ref, bf16[1024,512]{1,0:T(8,128)(2,1)} %collective-permute-done.16.refs_0_, bf16[1024,512]{1,0:T(8,128)(2,1)} %collective-permute-done.17.refs_1_, ...), custom_call_target="tpu_custom_call" | custom-call | flops 4294967296 | bytes 16777216 | tf_op jit(solution)/shard_map/project/pallas_call | solution.py:162
  183.7 1.0 copy-done.6
  184.7 7.3 %project.15.q_ref = bf16[1024,512]{1,0:T(8,128)(2,1)} custom-call(s32[4]{0:T(128)} %get-tuple-element.43.index_ref, bf16[32,1024,256]{2,1,0:T(8,128)(2,1)} %norm_rows.1.x_ref, bf16[1024,512]{1,0:T(8,128)(2,1)} %copy-done.6, f32[1024,512]{1,0:T(8,128)} %project.11.refs_1_, f32[1,512]{1,0:T(1,128)} %maximum_convert_fusion.1.refs_2_, ...), custom_call_target="tpu_custom_call" | custom-call | flops 1073741824 | bytes 7340032 | tf_op jit(solution)/shard_map/project/pallas_call | solution.py:162
  192.0 7.3 %project.13.q_ref = bf16[1024,512]{1,0:T(8,128)(2,1)} custom-call(s32[4]{0:T(128)} %get-tuple-element.57.index_ref, bf16[32,1024,256]{2,1,0:T(8,128)(2,1)} %norm_rows.1.x_ref, bf16[1024,512]{1,0:T(8,128)(2,1)} %collective-permute-done.15.refs_0_, f32[1024,512]{1,0:T(8,128)} %project.12.refs_1_, f32[1,512]{1,0:T(1,128)} %slice.24.refs_2_, ...), custom_call_target="tpu_custom_call" | custom-call | flops 1073741824 | bytes 7340032 | tf_op jit(solution)/shard_map/project/pallas_call | solution.py:162
  199.3 1.3 copy-done.5
  200.7 9.4 %project.14.text_ref = bf16[1024,256]{1,0:T(8,128)(2,1)} custom-call(s32[16]{0:T(128)} %iota_add_fusion.index_ref, bf16[32,1024,256]{2,1,0:T(8,128)(2,1)} %norm_rows.1.x_ref, bf16[4096,256]{1,0:T(8,128)(2,1)} %copy-done.5, f32[1024,256]{1,0:T(8,128)} %project.10.refs_1_, f32[1,256]{1,0:T(1,128)} %maximum_convert_fusion.2.refs_2_, ...), custom_call_target="tpu_custom_call" | custom-call | flops 2147483648 | bytes 12582912 | tf_op jit(solution)/shard_map/project/pallas_call | solution.py:162
  210.1 16.3 %attend.2.refs_0_ = bf16[1024,1024]{1,0:T(8,128)(2,1)} custom-call(s32[16]{0:T(128)} %add_clamp_fusion.which_ref, s32[16]{0:T(128)} %len_ref.3, bf16[1024,512]{1,0:T(8,128)(2,1)} %project.15.q_ref, bf16[1024,256]{1,0:T(8,128)(2,1)} %project.14.text_ref, bf16[32,2,32,256]{3,2,1,0:T(8,128)(2,1)} %all-to-all-done.1.visual_ref), custom_call_target="tpu_custom_call" | custom-call | flops 2147483648 | bytes 2097152 | tf_op jit(solution)/shard_map/attend/pallas_call | solution.py:234
  226.4 16.2 %attend.3 = bf16[1024,1024]{1,0:T(8,128)(2,1)} custom-call(s32[16]{0:T(128)} %add_clamp_fusion.which_ref, s32[16]{0:T(128)} %len_ref.3, bf16[1024,512]{1,0:T(8,128)(2,1)} %project.13.q_ref, bf16[1024,256]{1,0:T(8,128)(2,1)} %project.14.text_ref, bf16[32,2,32,256]{3,2,1,0:T(8,128)(2,1)} %all-to-all-done.1.visual_ref, ...), custom_call_target="tpu_custom_call", output_to_operand_aliasing={{}: (5, {})} | custom-call | flops 2147483648 | bytes 2097152 | tf_op jit(solution)/shard_map/attend/pallas_call | solution.py:234
  (62 shorter events, 0.3 us)
Async XLA Ops:
  6.5 85.1 %copy-start = (s32[32]{0:T(128)S(1)}, s32[32]{0:T(128)}, u32[]{:S(2)}) copy-start(s32[32]{0:T(128)} %param.20) | copy-start | bytes 388
  6.5 91.9 %all-gather.3.cloned.1.call-start = ((), (), s32[]{:S(2)}) async-start(), calls=%async_computation.2 | async-start | bytes 2228224 | tf_op jit(solution)/shard_map/all_gather | solution.py:292
  7.3 20.6 %copy-start.10 = (s32[4]{0:T(128)S(1)}, s32[4]{0:T(128)}, u32[]{:S(2)}) copy-start(s32[4]{0:T(128)} %constant.153.clone) | copy-start | bytes 52
  8.3 20.7 %collective-permute-start.3 = (bf16[256,512]{1,0:T(8,128)(2,1)S(1)}, bf16[256,512]{1,0:T(8,128)(2,1)S(1)}, u32[]{:S(2)}, u32[]{:S(2)}) collective-permute-start(bf16[256,512]{1,0:T(8,128)(2,1)S(1)} %get-tuple-element.50), channel_id=1, source_target_pairs={{0,16},{16,32},{32,48},{48,0},{1,17},{17,33},{33,49},{49,1},{2,18}... | collective-permute-start | bytes 786440 | tf_op jit(solution)/shard_map/ppermute | solution.py:29
  10.0 22.0 %collective-permute-start.4 = (bf16[256,512]{1,0:T(8,128)(2,1)S(1)}, bf16[256,512]{1,0:T(8,128)(2,1)S(1)}, u32[]{:S(2)}, u32[]{:S(2)}) collective-permute-start(bf16[256,512]{1,0:T(8,128)(2,1)S(1)} %get-tuple-element.50), channel_id=1, source_target_pairs={{0,48},{16,0},{32,16},{48,32},{1,49},{17,1},{33,17},{49,33},{2,50}... | collective-permute-start | bytes 786440 | tf_op jit(solution)/shard_map/ppermute | solution.py:29
  11.7 22.2 %collective-permute-start.5 = (bf16[256,512]{1,0:T(8,128)(2,1)S(1)}, bf16[256,512]{1,0:T(8,128)(2,1)S(1)}, u32[]{:S(2)}, u32[]{:S(2)}) collective-permute-start(bf16[256,512]{1,0:T(8,128)(2,1)S(1)} %get-tuple-element.50), channel_id=1, source_target_pairs={{0,32},{16,48},{32,0},{48,16},{1,33},{17,49},{33,1},{49,17},{2,34}... | collective-permute-start | bytes 786440 | tf_op jit(solution)/shard_map/ppermute | solution.py:29
  13.5 21.1 %collective-permute-start = (bf16[256,512]{1,0:T(8,128)(2,1)S(1)}, bf16[256,512]{1,0:T(8,128)(2,1)S(1)}, u32[]{:S(2)}, u32[]{:S(2)}) collective-permute-start(bf16[256,512]{1,0:T(8,128)(2,1)S(1)} %get-tuple-element.51), channel_id=1, source_target_pairs={{0,4},{4,8},{8,12},{12,0},{1,5},{5,9},{9,13},{13,1},{2,6},{6,10},{... | collective-permute-start | bytes 786440 | tf_op jit(solution)/shard_map/ppermute | solution.py:29
  15.1 19.5 %collective-permute-start.1 = (bf16[256,512]{1,0:T(8,128)(2,1)S(1)}, bf16[256,512]{1,0:T(8,128)(2,1)S(1)}, u32[]{:S(2)}, u32[]{:S(2)}) collective-permute-start(bf16[256,512]{1,0:T(8,128)(2,1)S(1)} %get-tuple-element.51), channel_id=1, source_target_pairs={{0,12},{4,0},{8,4},{12,8},{1,13},{5,1},{9,5},{13,9},{2,14},{6,2},{... | collective-permute-start | bytes 786440 | tf_op jit(solution)/shard_map/ppermute | solution.py:29
  18.8 79.7 %all-to-all-start = ((bf16[128,8,256]{2,1,0:T(8,128)(2,1)}), bf16[128,8,256]{2,1,0:T(8,128)(2,1)}, u32[]{:S(2)}, u32[]{:S(2)}) async-start(bf16[128,8,256]{2,1,0:T(8,128)(2,1)} %bitcast.8), calls=%async_computation | async-start | bytes 1048576 | tf_op jit(solution)/shard_map/all_to_all | solution.py:305
  29.0 14.2 %collective-permute-start.2 = (bf16[256,512]{1,0:T(8,128)(2,1)S(1)}, bf16[256,512]{1,0:T(8,128)(2,1)S(1)}, u32[]{:S(2)}, u32[]{:S(2)}) collective-permute-start(bf16[256,512]{1,0:T(8,128)(2,1)S(1)} %get-tuple-element.51), channel_id=1, source_target_pairs={{0,8},{4,12},{8,0},{12,4},{1,9},{5,13},{9,1},{13,5},{2,10},{6,14},... | collective-permute-start | bytes 786440 | tf_op jit(solution)/shard_map/ppermute | solution.py:29
  32.0 30.7 %copy-start.7 = (bf16[8192]{0:T(1024)(128)(2,1)S(1)}, bf16[8192]{0:T(1024)(128)(2,1)}, u32[]{:S(2)}) copy-start(bf16[8192]{0:T(1024)(128)(2,1)} %param.12) | copy-start | bytes 49156
  32.0 12.7 %collective-permute-start.6 = (bf16[256,512]{1,0:T(8,128)(2,1)S(1)}, bf16[256,512]{1,0:T(8,128)(2,1)S(1)}, u32[]{:S(2)}, u32[]{:S(2)}) collective-permute-start(bf16[256,512]{1,0:T(8,128)(2,1)S(1)} %get-tuple-element.50), channel_id=1, source_target_pairs={{0,64},{64,0},{1,65},{65,1},{2,66},{66,2},{3,67},{67,3},{4,68},{68... | collective-permute-start | bytes 786440 | tf_op jit(solution)/shard_map/ppermute | solution.py:29
  33.9 49.3 %copy-start.2 = (bf16[1024,512]{1,0:T(8,128)(2,1)}, bf16[1024,512]{1,0:T(8,128)(2,1)S(1)}, u32[]{:S(2)}) copy-start(bf16[1024,512]{1,0:T(8,128)(2,1)S(1)} %pad_maximum_fusion.1.refs_0_) | copy-start | bytes 3145732
  33.9 55.0 %collective-permute-start.13 = (bf16[1024,512]{1,0:T(8,128)(2,1)S(1)}, bf16[1024,512]{1,0:T(8,128)(2,1)}, u32[]{:S(2)}, u32[]{:S(2)}) collective-permute-start(bf16[1024,512]{1,0:T(8,128)(2,1)S(1)} %pad_maximum_fusion.1.refs_0_), channel_id=1, source_target_pairs={{0,4},{4,8},{8,12},{12,0},{1,5},{5,9},{9,13},{13,1},{2,6},{6,10},{... | collective-permute-start | bytes 3145736 | tf_op jit(solution)/shard_map/ppermute | solution.py:29
  43.2 40.0 %copy-start.3 = (bf16[1024,512]{1,0:T(8,128)(2,1)}, bf16[1024,512]{1,0:T(8,128)(2,1)S(1)}, u32[]{:S(2)}) copy-start(bf16[1024,512]{1,0:T(8,128)(2,1)S(1)} %pad_maximum_fusion.refs_0_) | copy-start | bytes 3145732
  43.3 45.5 %collective-permute-start.17 = (bf16[1024,512]{1,0:T(8,128)(2,1)S(1)}, bf16[1024,512]{1,0:T(8,128)(2,1)}, u32[]{:S(2)}, u32[]{:S(2)}) collective-permute-start(bf16[1024,512]{1,0:T(8,128)(2,1)S(1)} %pad_maximum_fusion.refs_0_), channel_id=1, source_target_pairs={{0,64},{64,0},{1,65},{65,1},{2,66},{66,2},{3,67},{67,3},{4,68},{68... | collective-permute-start | bytes 3145736 | tf_op jit(solution)/shard_map/ppermute | solution.py:29
  44.8 12.7 %collective-permute-start.7 = (bf16[256,512]{1,0:T(8,128)(2,1)S(1)}, bf16[256,512]{1,0:T(8,128)(2,1)S(1)}, u32[]{:S(2)}, u32[]{:S(2)}) collective-permute-start(bf16[256,512]{1,0:T(8,128)(2,1)S(1)} %collective-permute-done.6), channel_id=1, source_target_pairs={{0,16},{16,32},{32,48},{48,0},{1,17},{17,33},{33,49},{49,1},{2,18}... | collective-permute-start | bytes 786440 | tf_op jit(solution)/shard_map/ppermute | solution.py:29
  45.8 16.3 %collective-permute-start.8 = (bf16[256,512]{1,0:T(8,128)(2,1)S(1)}, bf16[256,512]{1,0:T(8,128)(2,1)S(1)}, u32[]{:S(2)}, u32[]{:S(2)}) collective-permute-start(bf16[256,512]{1,0:T(8,128)(2,1)S(1)} %collective-permute-done.6), channel_id=1, source_target_pairs={{0,48},{16,0},{32,16},{48,32},{1,49},{17,1},{33,17},{49,33},{2,50}... | collective-permute-start | bytes 786440 | tf_op jit(solution)/shard_map/ppermute | solution.py:29
  48.6 34.6 %collective-permute-start.9 = (bf16[256,512]{1,0:T(8,128)(2,1)S(1)}, bf16[256,512]{1,0:T(8,128)(2,1)}, u32[]{:S(2)}, u32[]{:S(2)}) collective-permute-start(bf16[256,512]{1,0:T(8,128)(2,1)S(1)} %collective-permute-done.6), channel_id=1, source_target_pairs={{0,32},{16,48},{32,0},{48,16},{1,33},{17,49},{33,1},{49,17},{2,34}... | collective-permute-start | bytes 786440 | tf_op jit(solution)/shard_map/ppermute | solution.py:29
  57.5 36.3 %collective-permute-start.14 = (bf16[1024,512]{1,0:T(8,128)(2,1)S(1)}, bf16[1024,512]{1,0:T(8,128)(2,1)}, u32[]{:S(2)}, u32[]{:S(2)}) collective-permute-start(bf16[1024,512]{1,0:T(8,128)(2,1)S(1)} %pad_maximum_fusion.1.refs_0_), channel_id=1, source_target_pairs={{0,12},{4,0},{8,4},{12,8},{1,13},{5,1},{9,5},{13,9},{2,14},{6,2},{... | collective-permute-start | bytes 3145736 | tf_op jit(solution)/shard_map/ppermute | solution.py:29
  62.2 33.7 %collective-permute-start.11 = (bf16[1024,512]{1,0:T(8,128)(2,1)S(1)}, bf16[1024,512]{1,0:T(8,128)(2,1)}, u32[]{:S(2)}, u32[]{:S(2)}) collective-permute-start(bf16[1024,512]{1,0:T(8,128)(2,1)S(1)} %pad_maximum_fusion.refs_0_), channel_id=1, source_target_pairs={{0,16},{16,32},{32,48},{48,0},{1,17},{17,33},{33,49},{49,1},{2,18}... | collective-permute-start | bytes 3145736 | tf_op jit(solution)/shard_map/ppermute | solution.py:29
  83.2 8.4 %copy-start.9 = (bf16[1024]{0:T(1024)(128)(2,1)S(1)}, bf16[1024]{0:T(1024)(128)(2,1)}, u32[]{:S(2)}) copy-start(bf16[1024]{0:T(1024)(128)(2,1)} %param.14) | copy-start | bytes 6148
  83.2 9.9 %copy-start.8 = (bf16[1,256]{1,0:T(2,128)(2,1)S(1)}, bf16[1,256]{1,0:T(2,128)(2,1)}, u32[]{:S(2)}) copy-start(bf16[1,256]{1,0:T(2,128)(2,1)} %param.16) | copy-start | bytes 1540
  83.2 28.1 %collective-permute-start.12 = (bf16[1024,512]{1,0:T(8,128)(2,1)S(1)}, bf16[1024,512]{1,0:T(8,128)(2,1)}, u32[]{:S(2)}, u32[]{:S(2)}) collective-permute-start(bf16[1024,512]{1,0:T(8,128)(2,1)S(1)} %pad_maximum_fusion.refs_0_), channel_id=1, source_target_pairs={{0,48},{16,0},{32,16},{48,32},{1,49},{17,1},{33,17},{49,33},{2,50}... | collective-permute-start | bytes 3145736 | tf_op jit(solution)/shard_map/ppermute | solution.py:29
  88.8 43.8 %copy-start.4 = (bf16[1024,512]{1,0:T(8,128)(2,1)}, bf16[1024,512]{1,0:T(8,128)(2,1)S(1)}, u32[]{:S(2)}) copy-start(bf16[1024,512]{1,0:T(8,128)(2,1)S(1)} %pad_maximum_fusion.2.refs_1_) | copy-start | bytes 3145732
  88.8 24.6 %collective-permute-start.10 = (bf16[1024,512]{1,0:T(8,128)(2,1)S(1)}, bf16[1024,512]{1,0:T(8,128)(2,1)}, u32[]{:S(2)}, u32[]{:S(2)}) collective-permute-start(bf16[1024,512]{1,0:T(8,128)(2,1)S(1)} %pad_maximum_fusion.2.refs_1_), channel_id=1, source_target_pairs={{0,12},{4,0},{8,4},{12,8},{1,13},{5,1},{9,5},{13,9},{2,14},{6,2},{... | collective-permute-start | bytes 3145736 | tf_op jit(solution)/shard_map/ppermute | solution.py:29
  88.9 35.2 %collective-permute-start.19 = (bf16[1024,512]{1,0:T(8,128)(2,1)}, bf16[1024,512]{1,0:T(8,128)(2,1)}, u32[]{:S(2)}, u32[]{:S(2)}) collective-permute-start(bf16[1024,512]{1,0:T(8,128)(2,1)} %collective-permute-done.17.refs_1_), channel_id=1, source_target_pairs={{0,48},{16,0},{32,16},{48,32},{1,49},{17,1},{33,17},{49,33},{2,50}... | collective-permute-start | bytes 3145736 | tf_op jit(solution)/shard_map/ppermute | solution.py:29
  93.8 54.2 %collective-permute-start.21 = (bf16[1024,512]{1,0:T(8,128)(2,1)S(1)}, bf16[1024,512]{1,0:T(8,128)(2,1)}, u32[]{:S(2)}, u32[]{:S(2)}) collective-permute-start(bf16[1024,512]{1,0:T(8,128)(2,1)S(1)} %pad_maximum_fusion.2.refs_1_), channel_id=1, source_target_pairs={{0,4},{4,8},{8,12},{12,0},{1,5},{5,9},{9,13},{13,1},{2,6},{6,10},{... | collective-permute-start | bytes 3145736 | tf_op jit(solution)/shard_map/ppermute | solution.py:29
  95.8 56.0 %collective-permute-start.20 = (bf16[1024,512]{1,0:T(8,128)(2,1)}, bf16[1024,512]{1,0:T(8,128)(2,1)}, u32[]{:S(2)}, u32[]{:S(2)}) collective-permute-start(bf16[1024,512]{1,0:T(8,128)(2,1)} %collective-permute-done.13.refs_1_), channel_id=1, source_target_pairs={{0,4},{4,8},{8,12},{12,0},{1,5},{5,9},{9,13},{13,1},{2,6},{6,10},{... | collective-permute-start | bytes 3145736 | tf_op jit(solution)/shard_map/ppermute | solution.py:29
  111.4 49.7 %collective-permute-start.18 = (bf16[1024,512]{1,0:T(8,128)(2,1)}, bf16[1024,512]{1,0:T(8,128)(2,1)}, u32[]{:S(2)}, u32[]{:S(2)}) collective-permute-start(bf16[1024,512]{1,0:T(8,128)(2,1)} %collective-permute-done.17.refs_1_), channel_id=1, source_target_pairs={{0,16},{16,32},{32,48},{48,0},{1,17},{17,33},{33,49},{49,1},{2,18}... | collective-permute-start | bytes 3145736 | tf_op jit(solution)/shard_map/ppermute | solution.py:29
  113.4 47.7 %collective-permute-start.16 = (bf16[1024,512]{1,0:T(8,128)(2,1)}, bf16[1024,512]{1,0:T(8,128)(2,1)}, u32[]{:S(2)}, u32[]{:S(2)}) collective-permute-start(bf16[1024,512]{1,0:T(8,128)(2,1)} %collective-permute-done.11.refs_1_), channel_id=1, source_target_pairs={{0,16},{16,32},{32,48},{48,0},{1,17},{17,33},{33,49},{49,1},{2,18}... | collective-permute-start | bytes 3145736 | tf_op jit(solution)/shard_map/ppermute | solution.py:29
  124.1 75.2 %collective-permute-start.22 = (bf16[4096,256]{1,0:T(8,128)(2,1)}, bf16[4096,256]{1,0:T(8,128)(2,1)S(1)}, u32[]{:S(2)}, u32[]{:S(2)}) collective-permute-start(bf16[4096,256]{1,0:T(8,128)(2,1)} %bitcast.21), channel_id=1, source_target_pairs={{0,64},{64,0},{1,65},{65,1},{2,66},{66,2},{3,67},{67,3},{4,68},{68... | collective-permute-start | bytes 6291464 | tf_op jit(solution)/shard_map/ppermute | solution.py:29
  148.1 35.6 %collective-permute-start.23 = (bf16[1024,512]{1,0:T(8,128)(2,1)}, bf16[1024,512]{1,0:T(8,128)(2,1)S(1)}, u32[]{:S(2)}, u32[]{:S(2)}) collective-permute-start(bf16[1024,512]{1,0:T(8,128)(2,1)} %collective-permute-done.19.refs_3_), channel_id=1, source_target_pairs={{0,48},{16,0},{32,16},{48,32},{1,49},{17,1},{33,17},{49,33},{2,50}... | collective-permute-start | bytes 3145736 | tf_op jit(solution)/shard_map/ppermute | solution.py:29
  151.8 31.9 %collective-permute-start.15 = (bf16[1024,512]{1,0:T(8,128)(2,1)}, bf16[1024,512]{1,0:T(8,128)(2,1)}, u32[]{:S(2)}, u32[]{:S(2)}) collective-permute-start(bf16[1024,512]{1,0:T(8,128)(2,1)} %collective-permute-done.10.refs_3_), channel_id=1, source_target_pairs={{0,12},{4,0},{8,4},{12,8},{1,13},{5,1},{9,5},{13,9},{2,14},{6,2},{... | collective-permute-start | bytes 3145736 | tf_op jit(solution)/shard_map/ppermute | solution.py:29
  153.4 7.1 %copy-start.11 = (s32[16]{0:T(128)S(1)}, s32[16]{0:T(128)}, u32[]{:S(2)}) copy-start(s32[16]{0:T(128)} %param.18) | copy-start | bytes 196
  154.9 28.7 %all-to-all-start.1 = ((bf16[32,2,32,256]{3,2,1,0:T(8,128)(2,1)}), bf16[32,2,32,256]{3,2,1,0:T(8,128)(2,1)}, u32[]{:S(2)}, u32[]{:S(2)}) async-start(bf16[32,2,32,256]{3,2,1,0:T(8,128)(2,1)} %copy.27), calls=%async_computation.1 | async-start | bytes 2097152 | tf_op jit(solution)/shard_map/all_to_all | solution.py:327
  183.7 1.0 copy-start.6
  199.3 1.3 copy-start.5
  210.1 32.5 %copy-start.1 = (s32[32]{0:T(128)S(1)}, s32[32]{0:T(128)}, u32[]{:S(2)}) copy-start(s32[32]{0:T(128)} %param.20) | copy-start | bytes 388
Sparse Core Ops, SparseCore 0:
  9.5 62.3 all-gather.2
